TPU v7x, 128 devices: a whole 4x4x4 slice. The times are simulated.
128 devices in a mesh: row: 8 (over z, core), col: 16 (over x, y).
Axes of the slice: x: 4, y: 4, z: 4, core: 2. Of those that a mesh axis runs over, the one named last changes fastest.
Arguments:
- kernel: float32 [8, 8, 256, 4, 16, 256], P(None, 'row', None, None, 'col'), as said below
Outputs:
- factored: float32 [8, 8, 256, 4, 16, 256], P(None, 'row', None, None, 'col')
Inputs may be any that keep to these rules, and one draw needn't show every extreme that they name: kernel read as the 16384 by 16384 matrix is symmetric and positive definite, with every diagonal entry equal to 2 and every other entry in (0, 1].
All inputs are finite; a program needn't handle non-finite values.
Results may differ from a plain program's by a relative error of at most 0.0001.
Values sent between devices are 32-bit elements; how exact they have to be, the bound alone decides.
No kernel may reach another device: no remote copies, remote signals or barrier semaphores. Data moves between devices by JAX's collectives and lax.ppermute only.
A program may use at most 128 MiB of HBM per device.

v0:
```python
import jax
import jax.numpy as jnp
from jax import lax
from jax.sharding import PartitionSpec as P


def broadcast(array, axis, root):
    mine = lax.axis_index(axis) == root
    return lax.psum(jnp.where(mine, array, jnp.zeros_like(array)), axis)


def panel_factor(blocks, panel_index, row_index, col_index, row_count, col_count):
    tile_rows, width, tile_cols = (blocks.shape[0], blocks.shape[1], blocks.shape[2])
    taken = blocks[:, :, panel_index // col_count, :]
    received = broadcast(taken, "col", panel_index % col_count)
    diagonal = broadcast(received[panel_index // row_count], "row", panel_index % row_count)
    factor = jnp.tril(jnp.linalg.cholesky(diagonal))
    solved = jax.scipy.linalg.solve_triangular(
        factor, received.reshape(tile_rows * width, width).T, lower=True
    ).T
    solved = solved.reshape(tile_rows, width, width)
    global_rows = (jnp.arange(tile_rows) * row_count + row_index)[:, None, None]
    lower_rows = jnp.where(global_rows > panel_index, solved, jnp.float32(0.0))
    column = jnp.where(global_rows == panel_index, factor[None], lower_rows)
    stride = col_count // row_count
    grouped = lower_rows.reshape(tile_cols, stride, width, width)
    chosen = lax.dynamic_index_in_dim(grouped, col_index // row_count, axis=1, keepdims=False)
    col_tiles = broadcast(chosen, "row", col_index % row_count)
    return (lower_rows, col_tiles, column)


def subtract(blocks, lower_rows, col_tiles):
    tile_rows, width, tile_cols = (blocks.shape[0], blocks.shape[1], blocks.shape[2])
    left_side = lower_rows.reshape(tile_rows * width, -1)
    right_side = col_tiles.reshape(tile_cols * width, -1)
    product = jnp.dot(left_side, right_side.T, precision=lax.Precision.HIGHEST)
    return blocks - product.reshape(tile_rows, width, tile_cols, width)


def settle(blocks, panel_index, column, global_rows, global_cols):
    blocks = jnp.where(global_cols == panel_index, column[:, :, None, :], blocks)
    return jnp.where(
        (global_rows == panel_index) & (global_cols > panel_index), jnp.float32(0.0), blocks
    )


def shards(kernel):
    tile_rows, width, tile_cols = (kernel.shape[0], kernel.shape[2], kernel.shape[3])
    blocks = kernel.reshape(tile_rows, width, tile_cols, width)
    row_count = lax.axis_size("row")
    col_count = lax.axis_size("col")
    row_index = lax.axis_index("row")
    col_index = lax.axis_index("col")
    global_rows = (jnp.arange(tile_rows) * row_count + row_index).reshape(tile_rows, 1, 1, 1)
    global_cols = (jnp.arange(tile_cols) * col_count + col_index).reshape(1, 1, tile_cols, 1)
    rows_first, cols_first, column_first = panel_factor(
        blocks, 0, row_index, col_index, row_count, col_count
    )
    blocks = settle(
        subtract(blocks, rows_first, cols_first), 0, column_first, global_rows, global_cols
    )
    rows_second, cols_second, column_second = panel_factor(
        blocks, 1, row_index, col_index, row_count, col_count
    )
    blocks = subtract(blocks, rows_second, cols_second)
    blocks = settle(blocks, 1, column_second, global_rows, global_cols)
    return blocks.reshape(kernel.shape)


def solution(mesh):
    placed = (P(None, "row", None, None, "col", None),)
    return jax.shard_map(
        shards,
        mesh=mesh,
        in_specs=placed,
        out_specs=P(None, "row", None, None, "col", None),
        check_vma=False,
    )
```

profile of v0, /device:TPU:1, one launch (start us, length us, event | category | flops | bytes accessed | tf_op | source)
XLA Modules:
  0.0 675.8 jit_solution(1418619541041152447)
XLA Ops:
  6.5 20.5 %copy.16 = f32[8,1,256,4,1,256]{2,5,0,3,4,1:T(8,128)} copy(f32[8,1,256,4,1,256]{5,4,3,2,1,0:T(1,128)} %param.4) | data formatting | bytes 16777216 | tf_op args[0]
  27.0 3.1 fusion.3
  30.8 91.7 %all-reduce.8.cloned.1.call-done = f32[8,256,256]{1,2,0:T(8,128)} async-done(((f32[8,256,256]{1,2,0:T(8,128)}), f32[8,256,256]{1,2,0:T(8,128)}) %all-reduce.8.cloned.1.call-update) | async-done | bytes 2097168 | tf_op jit(solution)/shard_map/psum | solution.py:9
  126.8 56.6 %all-reduce.10.cloned.1.call-done = f32[256,256]{0,1:T(8,128)} async-done(((f32[256,256]{0,1:T(8,128)}), f32[256,256]{0,1:T(8,128)}) %all-reduce.10.cloned.1.call-update) | async-done | bytes 262160 | tf_op jit(solution)/shard_map/psum | solution.py:9
  185.5 11.7 %cholesky.130 = f32[128,128]{1,0:T(8,128)S(1)} custom-call(f32[128,128]{1,0:T(8,128)S(1)} %cholesky.194), custom_call_target="Cholesky" | custom-call | tf_op jit(solution)/shard_map/jit(cholesky)/cholesky | solution.py:17
  197.3 9.8 %custom-call.13 = f32[1,128,128]{1,2,0:T(8,128)S(1)} custom-call(f32[1,128,128]{2,1,0:T(8,128)S(1)} %get-tuple-element.58), custom_call_target="InvertDiagBlocksLowerTriangular" | custom-call | tf_op jit(solution)/shard_map/jit(cholesky)/cholesky | solution.py:17
  207.6 11.7 %cholesky.147 = f32[128,128]{1,0:T(8,128)S(1)} custom-call(f32[128,128]{1,0:T(8,128)S(1)} %convolution_subtract_fusion.3), custom_call_target="Cholesky" | custom-call | tf_op jit(solution)/shard_map/jit(cholesky)/cholesky | solution.py:17
  222.0 3.7 while.4
  226.3 19.8 %custom-call.14 = f32[2,128,128]{1,2,0:T(8,128)S(1)} custom-call(f32[2,128,128]{2,1,0:T(8,128)S(1)} %get-tuple-element.21), custom_call_target="InvertDiagBlocksLowerTriangular" | custom-call | tf_op jit(solution)/shard_map/jit(_solve_triangular)/triangular_solve | solution.py:18
  250.1 2.5 fusion.33
  252.6 4.0 reshape.213
  256.6 2.5 constant_dynamic-slice_fusion.5
  261.2 2.4 select_bitcast_fusion.2
  265.3 2.9 copy.36
  270.1 55.4 %all-reduce.12.cloned.1.call-done = f32[4,256,256]{2,1,0:T(8,128)} async-done(((f32[4,256,256]{2,1,0:T(8,128)}), f32[4,256,256]{2,1,0:T(8,128)}) %all-reduce.12.cloned.1.call-update) | async-done | bytes 1048592 | tf_op jit(solution)/shard_map/psum | solution.py:9
  325.5 11.4 %select_select_fusion = f32[8,256,4,256]{1,3,0,2:T(8,128)S(1)} fusion(f32[8,256,256]{1,2,0:T(8,128)S(1)} %fusion.1, pred[4]{0:T(512)(128)(4,1)S(1)} %get-tuple-element.63, pred[8,4]{0,1:T(4,128)(4,1)S(1)} %broadcast_and_fusion, f32[8,256,256,1]{2,1,0,3:T(8,128)} %bitcast.129, f32[4,256,256]{2,1,0:T(8,128)} %all-reduce.12.cloned.1.call-done, ...), kind=kOutput, calls=%fused_computation.5 | convolution fusion | flops 6448742400 | bytes 22020132 | tf_op jit(solution)/shard_map/dot_general | solution.py:36
  336.9 3.4 copy-done
  342.5 89.6 %all-reduce.14.cloned.1.call-done = f32[8,256,256]{1,2,0:T(8,128)} async-done(((f32[8,256,256]{1,2,0:T(8,128)}), f32[8,256,256]{1,2,0:T(8,128)}) %all-reduce.14.cloned.1.call-update) | async-done | bytes 2097168 | tf_op jit(solution)/shard_map/psum | solution.py:9
  436.7 56.2 %all-reduce.16.cloned.1.call-done = f32[256,256]{0,1:T(8,128)} async-done(((f32[256,256]{0,1:T(8,128)}), f32[256,256]{0,1:T(8,128)}) %all-reduce.16.cloned.1.call-update) | async-done | bytes 262160 | tf_op jit(solution)/shard_map/psum | solution.py:9
  495.0 11.7 %cholesky.164 = f32[128,128]{1,0:T(8,128)S(1)} custom-call(f32[128,128]{1,0:T(8,128)S(1)} %cholesky.197), custom_call_target="Cholesky" | custom-call | tf_op jit(solution)/shard_map/jit(cholesky)/cholesky | solution.py:17
  506.8 9.8 %custom-call.15 = f32[1,128,128]{1,2,0:T(8,128)S(1)} custom-call(f32[1,128,128]{2,1,0:T(8,128)S(1)} %get-tuple-element.54), custom_call_target="InvertDiagBlocksLowerTriangular" | custom-call | tf_op jit(solution)/shard_map/jit(cholesky)/cholesky | solution.py:17
  517.1 11.7 %cholesky.181 = f32[128,128]{1,0:T(8,128)S(1)} custom-call(f32[128,128]{1,0:T(8,128)S(1)} %convolution_subtract_fusion.2), custom_call_target="Cholesky" | custom-call | tf_op jit(solution)/shard_map/jit(cholesky)/cholesky | solution.py:17
  532.2 4.0 while.5
  536.2 20.1 %custom-call.16 = f32[2,128,128]{1,2,0:T(8,128)S(1)} custom-call(f32[2,128,128]{2,1,0:T(8,128)S(1)} %get-tuple-element.22), custom_call_target="InvertDiagBlocksLowerTriangular" | custom-call | tf_op jit(solution)/shard_map/jit(_solve_triangular)/triangular_solve | solution.py:18
  560.3 2.5 fusion.32
  562.7 4.0 reshape.216
  566.7 2.5 constant_dynamic-slice_fusion.4
  571.4 2.4 select_bitcast_fusion.1
  575.4 2.9 copy.37
  580.2 55.4 %all-reduce.18.cloned.1.call-done = f32[4,256,256]{2,1,0:T(8,128)} async-done(((f32[4,256,256]{2,1,0:T(8,128)}), f32[4,256,256]{2,1,0:T(8,128)}) %all-reduce.18.cloned.1.call-update) | async-done | bytes 1048592 | tf_op jit(solution)/shard_map/psum | solution.py:9
  635.6 12.5 %select_bitcast_fusion = f32[8,1,256,4,1,256]{2,5,0,3,4,1:T(8,128)} fusion(f32[8,256,4,256]{1,3,0,2:T(8,128)} %copy-done, f32[8,256,256]{1,2,0:T(8,128)S(1)} %fusion, pred[4]{0:T(512)(128)(4,1)S(1)} %get-tuple-element.65, pred[8,4]{0,1:T(4,128)(4,1)S(1)} %broadcast_and_fusion.1, f32[8,256,256,1]{2,1,0,3:T(8,128)} %bitcast.130, ...), kind=kOutput, calls=%fused_computation.4 | convolution fusion | flops 6448742400 | bytes 22020132 | tf_op jit(solution)/shard_map/dot_general | solution.py:36
  648.1 20.7 %copy.31 = f32[8,1,256,4,1,256]{5,4,3,2,1,0:T(1,128)} copy(f32[8,1,256,4,1,256]{2,5,0,3,4,1:T(8,128)} %select_bitcast_fusion) | data formatting | bytes 16777216 | tf_op jit(solution)/shard_map/reshape | solution.py:67
  (103 shorter events, 47.9 us)
Async XLA Ops:
  6.5 115.9 %all-reduce.8.cloned.1.call-start = ((), (), s32[]{:S(2)}) async-start(), calls=%async_computation | async-start | bytes 4194304 | tf_op jit(solution)/shard_map/psum | solution.py:9
  30.2 153.3 %all-reduce.10.cloned.1.call-start = ((), (), s32[]{:S(2)}) async-start(), calls=%async_computation.1 | async-start | bytes 524288 | tf_op jit(solution)/shard_map/psum | solution.py:9
  30.2 0.5 copy-start.3
  124.2 201.3 %all-reduce.12.cloned.1.call-start = ((), (), s32[]{:S(2)}) async-start(), calls=%async_computation.2 | async-start | bytes 2097152 | tf_op jit(solution)/shard_map/psum | solution.py:9
  225.7 0.6 copy-start.9
  256.6 4.7 copy-start.8
  263.7 1.5 copy-start.2
  263.7 168.5 %all-reduce.14.cloned.1.call-start = ((), (), s32[]{:S(2)}) async-start(), calls=%async_computation.3 | async-start | bytes 4194304 | tf_op jit(solution)/shard_map/psum | solution.py:9
  265.3 2.9 copy-start.4
  336.9 3.4 copy-start
  341.8 151.1 %all-reduce.16.cloned.1.call-start = ((), (), s32[]{:S(2)}) async-start(), calls=%async_computation.4 | async-start | bytes 524288 | tf_op jit(solution)/shard_map/psum | solution.py:9
  341.9 0.6 copy-start.5
  433.8 201.8 %all-reduce.18.cloned.1.call-start = ((), (), s32[]{:S(2)}) async-start(), calls=%async_computation.5 | async-start | bytes 2097152 | tf_op jit(solution)/shard_map/psum | solution.py:9
  436.7 95.5 %copy-start.10 = (s32[2,2]{1,0:T(2,128)S(1)}, s32[2,2]{1,0:T(2,128)}, u32[]{:S(2)}) copy-start(s32[2,2]{1,0:T(2,128)} %copy-done.9) | copy-start | bytes 52
  566.7 4.6 copy-start.7
  573.8 1.5 copy-start.1
  575.4 2.9 copy-start.6
Sparse Core Ops, SparseCore 0:
  30.3 92.1 all-reduce.7
  124.9 58.4 all-reduce.9
  263.8 61.6 all-reduce.11
  341.9 90.1 all-reduce.13
  434.4 58.4 all-reduce.15
  573.9 61.6 all-reduce.17
where the time goes:
time: 687 us; the launch traced here: 676 us
  waiting for transfers between devices  405 us (59%)
  other arithmetic  136 us (20%)
  local copies, waits for them, and re-layouts  84.8 us (12%)
  matrix products  32.7 us (5%)
  between operations  16.5 us (2%)
    psum x6, waiting for transfers between devices, broadcast(): return lax.psum(jnp.where(mine, array, jnp.zeros_like(array)), axis)  405 us
    another operation x13, other arithmetic, panel_factor(): factor = jnp.tril(jnp.linalg.cholesky(diagonal))  68.6 us
    another operation x5, other arithmetic, panel_factor(): jax.scipy.linalg.solve_triangular(factor, received.reshape(tile_rows * wi...  41.4 us
    unnamed x25, local copies, waits for them, and re-layouts  29.8 us
    dot_general x2, matrix products, subtract(): product = jnp.dot(left_side, right_side.T, precision=lax.Precision.HIGHEST)  23.9 us
    reshape x1, local copies, waits for them, and re-layouts, shards(): return blocks.reshape(kernel.shape)  20.7 us
  transfers between devices with their start and end apart: 6, of which 6 were waited for; matrix products, arithmetic and copies ran while one was open for 3% of the time, Pallas kernels for 0%

commit v1 on v0

v1 whole, which is shorter than its diff:
```python
import jax
import jax.numpy as jnp
from jax import lax
from jax.experimental import pallas as pl
from jax.experimental.pallas import tpu as pltpu
from jax.sharding import PartitionSpec as P

F32 = jnp.float32
BF16 = jnp.bfloat16
ROWS, COLS = 8, 16
MIB = 1024 * 1024


def dot(a, b, ca, cb):
    return lax.dot_general(
        a,
        b,
        (((ca,), (cb,)), ((), ())),
        precision=lax.Precision.HIGHEST,
        preferred_element_type=F32,
    )


def matmul(a, b):
    return jnp.dot(a, b, preferred_element_type=F32)


def split(x):
    high = x.astype(BF16)
    return high, (x - high.astype(F32)).astype(BF16)


def prepare_kernel(x_ref, tile_ref, turned_ref):
    for m in range(4):
        for h in range(2):
            half = x_ref[pl.ds(2 * m + h, 256, stride=8), :]
            tile_ref[m, :, 128 * h : 128 * h + 128] = half
            turned_ref[m, 128 * h : 128 * h + 128, :] = half.T


def prepare(x):
    shape = jax.ShapeDtypeStruct((4, 256, 256), F32)
    return pl.pallas_call(
        prepare_kernel,
        grid=(1,),
        in_specs=[pl.BlockSpec((2048, 128), lambda i: (0, 0))],
        out_specs=[pl.BlockSpec((4, 256, 256), lambda i: (0, 0, 0))] * 2,
        out_shape=[shape, shape],
    )(x)


def inner(block):
    n = 16
    rows = [block[8 * j : 8 * j + 8, :] for j in range(n)]
    lane = lax.broadcasted_iota(jnp.int32, (8, 128), 1)
    sub = lax.broadcasted_iota(jnp.int32, (8, 128), 0)
    inv_rows = [jnp.where(lane == sub + 8 * j, 1.0, 0.0).astype(jnp.float32) for j in range(n)]
    full = lambda v: jnp.broadcast_to(v, (8, 128))
    us, ws = [], []
    for j in range(n):
        r, e = rows[j], inv_rows[j]
        cols = [full(r[:, 8 * j + c : 8 * j + c + 1]) for c in range(8)]
        a = [[full(cols[c][i : i + 1, :]) if i >= c else None for c in range(8)] for i in range(8)]
        l = [[None] * 8 for _ in range(8)]
        inv = [None] * 8
        for c in range(8):
            inv[c] = lax.rsqrt(a[c][c])
            for i in range(c + 1, 8):
                l[i][c] = a[i][c] * inv[c]
            for d in range(c + 1, 8):
                for i in range(d, 8):
                    a[i][d] = a[i][d] - l[i][c] * l[d][c]
        ru = [full(r[i : i + 1, :]) for i in range(8)]
        eu = [full(e[i : i + 1, :]) for i in range(8)]
        for c in range(8):
            ru[c] = ru[c] * inv[c]
            eu[c] = eu[c] * inv[c]
            for i in range(c + 1, 8):
                ru[i] = ru[i] - l[i][c] * ru[c]
                eu[i] = eu[i] - l[i][c] * eu[c]
        u, w = ru[0], eu[0]
        for c in range(1, 8):
            u = jnp.where(sub == c, ru[c], u)
            w = jnp.where(sub == c, eu[c], w)
        us.append(u)
        ws.append(w)
        for i in range(j + 1, n):
            ri, ei = rows[i], inv_rows[i]
            v = [full(ri[:, 8 * j + c : 8 * j + c + 1]) for c in range(8)]
            for c in range(8):
                v[c] = v[c] * inv[c]
                for d in range(c + 1, 8):
                    v[d] = v[d] - l[d][c] * v[c]
            for c in range(8):
                ri = ri - v[c] * ru[c]
                ei = ei - v[c] * eu[c]
            rows[i], inv_rows[i] = ri, ei
    return jnp.concatenate(us, axis=0), jnp.concatenate(ws, axis=0)

def factor_kernel(d_ref, lt_ref, w_ref, s):
    for j in range(16):
        for r in range(2):
            for c in range(2):
                s[256 * r + 16 * j : 256 * r + 16 * j + 16, 256 * c : 256 * c + 256] = d_ref[j, r, c]
    ri = lax.broadcasted_iota(jnp.int32, (512, 512), 0)
    ci = lax.broadcasted_iota(jnp.int32, (512, 512), 1)
    w_ref[...] = jnp.where(ri == ci, 1.0, 0.0).astype(F32)
    lane = lax.broadcasted_iota(jnp.int32, (128, 512), 1)
    r1 = lax.broadcasted_iota(jnp.int32, (128, 128), 0)
    c1 = lax.broadcasted_iota(jnp.int32, (128, 128), 1)

    @pl.loop(0, 4)
    def _(k):
        at = pl.multiple_of(k * 128, 128)
        u_kk, w_kk = inner(s[pl.ds(at, 128), pl.ds(at, 128)])
        u_kk = jnp.where(c1 >= r1, u_kk, 0.0)
        w_kk = jnp.where(c1 <= r1, w_kk, 0.0)
        u = dot(w_kk, s[pl.ds(at, 128), :], 1, 0)
        u = jnp.where(lane >= at + 128, u, 0.0)
        we = dot(w_kk, w_ref[pl.ds(at, 128), :], 1, 0)
        lt_ref[pl.ds(at, 128), :] = u
        lt_ref[pl.ds(at, 128), pl.ds(at, 128)] = u_kk
        s[...] -= dot(u, u, 0, 0)
        w_ref[...] -= dot(u, we, 0, 0)
        w_ref[pl.ds(at, 128), :] = we


def factor(d):
    shape = jax.ShapeDtypeStruct((512, 512), F32)
    return pl.pallas_call(
        factor_kernel,
        out_shape=[shape, shape],
        scratch_shapes=[pltpu.VMEM((512, 512), F32)],
        compiler_params=pltpu.CompilerParams(vmem_limit_bytes=16 * MIB),
        cost_estimate=pl.CostEstimate(flops=3 * 10**10, bytes_accessed=4 * MIB, transcendentals=0),
    )(d)


def update_kernel(
    place, x_ref, g0_ref, g1_ref, w_ref, lt_ref, mine_ref, other_ref, out_ref, wt3, bc3
):
    l = pl.program_id(0)
    row, col = place[0], place[1]

    @pl.when(l == 0)
    def _():
        w = w_ref[...]
        high, low = split(w.T)
        wt3[0:512, :] = high
        wt3[512:1024, :] = low
        high, low = split(w)
        is_first = lax.rem(row, 2) == 0
        for m in range(4):
            mine, other = mine_ref[m], other_ref[m]
            a0 = jnp.where(is_first, mine, other)
            a1 = jnp.where(is_first, other, mine)
            a0h, a0l = split(a0)
            a1h, a1l = split(a1)
            b0 = matmul(high[0:256, 0:256], a0h) + (
                matmul(high[0:256, 0:256], a0l) + matmul(low[0:256, 0:256], a0h)
            )
            ah = jnp.concatenate([a0h, a1h], axis=0)
            al = jnp.concatenate([a0l, a1l], axis=0)
            b1 = matmul(high[256:512], ah) + (matmul(high[256:512], al) + matmul(low[256:512], ah))
            bh, bl = split(jnp.concatenate([b0, b1], axis=0))
            bc3[0:512, 256 * m : 256 * m + 256] = bh
            bc3[512:1024, 256 * m : 256 * m + 256] = bl
            bc3[1024:1536, 256 * m : 256 * m + 256] = bh

    x0h, x0l = split(g0_ref[0])
    x1h, x1l = split(g1_ref[0])
    wh, wl = wt3[0:512, :], wt3[512:1024, :]
    b0 = matmul(x0h, wh[0:256, 0:256]) + (
        matmul(x0l, wh[0:256, 0:256]) + matmul(x0h, wl[0:256, 0:256])
    )
    xh = jnp.concatenate([x0h, x1h], axis=1)
    xl = jnp.concatenate([x0l, x1l], axis=1)
    b1 = matmul(xh, wh[:, 256:512]) + (matmul(xl, wh[:, 256:512]) + matmul(xh, wl[:, 256:512]))
    b = jnp.concatenate([b0, b1], axis=1)
    bh, bl = split(b)
    left = jnp.concatenate([bh, bh, bl], axis=1)
    for m in range(4):
        product = matmul(left, bc3[:, 256 * m : 256 * m + 256])
        for h in range(2):
            at = pl.ds(2 * m + h, 256, stride=8)
            out_ref[at, :] = x_ref[at, :] - product[:, 128 * h : 128 * h + 128]

    @pl.when(col <= 1)
    def _():
        for h in range(2):
            out_ref[pl.ds(h, 256, stride=8), :] = jnp.where(
                col == 0, b0[:, 128 * h : 128 * h + 128], b1[:, 128 * h : 128 * h + 128]
            )

    @pl.when((l == 0) & (row <= 1))
    def _():
        zero = jnp.zeros((256, 128), F32)
        for mh in range(2, 8):
            out_ref[pl.ds(mh, 256, stride=8), :] = zero
        first = lt_ref[0:256, 0:256].T
        second = lt_ref[256:512, 256:512].T
        for h in range(2):
            at = slice(128 * h, 128 * h + 128)
            value = jnp.where(
                row == 0,
                jnp.where(col == 0, first[:, at], zero),
                jnp.where(col == 0, b0[:, at], jnp.where(col == 1, second[:, at], zero)),
            )
            out_ref[pl.ds(h, 256, stride=8), :] = value


def position(row, l, k):
    q = 2 * (l // 2) + k
    x = (row // 4 + 2 * (l % 2) + q // 4) % 4
    y = (row % 4 + q % 4) % 4
    return 4 * x + y


def update(place, x, gathered, w, lt, mine, other):
    block = pl.BlockSpec((2048, 128), lambda l, place: (l, 0))
    whole = lambda *shape: pl.BlockSpec(shape, lambda l, place: (0,) * len(shape))
    return pl.pallas_call(
        update_kernel,
        grid_spec=pltpu.PrefetchScalarGridSpec(
            num_scalar_prefetch=1,
            grid=(8,),
            in_specs=[
                block,
                pl.BlockSpec((1, 256, 256), lambda l, place: (position(place[0], l, 0), 0, 0)),
                pl.BlockSpec((1, 256, 256), lambda l, place: (position(place[0], l, 1), 0, 0)),
                whole(512, 512),
                whole(512, 512),
                whole(4, 256, 256),
                whole(4, 256, 256),
            ],
            out_specs=block,
            scratch_shapes=[pltpu.VMEM((1024, 512), BF16), pltpu.VMEM((1536, 1024), BF16)],
        ),
        out_shape=jax.ShapeDtypeStruct((16384, 128), F32),
        compiler_params=pltpu.CompilerParams(vmem_limit_bytes=48 * MIB),
    )(place, x, gathered, gathered, w, lt, mine, other)


def scatter_pairs(m):
    pairs = []
    for k in range(2):
        for c in range(COLS):
            row = c % ROWS
            target = position(row, 2 * m + c // ROWS, k)
            pairs.append((k * COLS + c, row * COLS + target))
    return pairs


def shards(kernel):
    row, col = lax.axis_index("row"), lax.axis_index("col")
    x = kernel.reshape(16384, 128)
    tile, turned = prepare(x)

    both = ("row", "col")
    share = sum(lax.ppermute(turned[m], both, scatter_pairs(m)) for m in range(4))
    gathered = lax.all_gather(share, "col")

    came = [
        lax.ppermute(tile, "row", [(k, 2 * z + k) for k in range(2)]) for z in (1, 3, 2)
    ]
    d = lax.all_to_all(tile[0].reshape(16, 16, 256), "col", 0, 0, tiled=True)[0:2]
    d = jnp.broadcast_to(d[None], (8, 2, 16, 256))
    d = lax.all_to_all(d, "row", 0, 0, tiled=True)[0:2]
    d = jnp.broadcast_to(d[None], (16, 2, 2, 16, 256))
    d = lax.all_to_all(d, "col", 0, 0, tiled=True)
    lt, w = factor(d)

    came, lt, w = lax.optimization_barrier((came, lt, w))
    mine = jnp.where(row < 2, tile, sum(came))
    other = lax.ppermute(mine, "row", [(r, r ^ 1) for r in range(ROWS)])
    place = jnp.stack([row, col]).astype(jnp.int32)
    return update(place, x, gathered, w, lt, mine, other).reshape(kernel.shape)


def solution(mesh):
    placed = P(None, "row", None, None, "col", None)
    return jax.shard_map(
        shards, mesh=mesh, in_specs=(placed,), out_specs=placed, check_vma=False
    )
```

time: 687 us -> 153 us (0.22); the launches traced: 676 us -> 153 us
  waiting for transfers between devices: 405 us -> 26.2 us
  other arithmetic: 136 us -> 3.3 us
  local copies, waits for them, and re-layouts: 84.8 us -> 3.37 us
  Pallas kernels: 0 us -> 50.2 us
  matrix products: 32.7 us -> 0 us
  starting transfers between devices: 0.21 us -> 31.5 us
  blocking collectives: 0 us -> 24.7 us
    psum x6 -> x0, waiting for transfers between devices: 405 us -> none  [broadcast(): return lax.psum(jnp.where(mine, array, jnp.zeros_like(array)), axis)]
    another operation x18 -> x1, other arithmetic: 110 us -> 0.07 us  [shards(): place = jnp.stack([row, col]).astype(jnp.int32)]
    pallas_call x0 -> x3, Pallas kernels: none -> 50.2 us  [the longest x1 28.6 us: factor(): pl.pallas_call(factor_kernel, out_shape=[shape, shape], scratch_shapes=[p...]
    unnamed x25 -> x0, local copies, waits for them, and re-layouts: 29.8 us -> none
    reshape x3 -> x0, local copies, waits for them, and re-layouts: 28.7 us -> none  [the longest x1 20.7 us: shards(): return blocks.reshape(kernel.shape)]
    ppermute x0 -> x8, starting transfers between devices: none -> 27.6 us  [the longest x4 16.4 us: shards(): lax.ppermute(turned[m], both, scatter_pairs(m))]
    all_to_all x0 -> x2, blocking collectives: none -> 24.7 us  [the longest x1 14.3 us: shards(): lax.all_to_all(tile[0].reshape(16, 16, 256), 'col', 0, 0, tiled=True)[0:2]]
    dot_general x2 -> x0, matrix products: 23.9 us -> none  [subtract(): product = jnp.dot(left_side, right_side.T, precision=lax.Precision.HIGHEST)]
  transfers between devices with their start and end apart: 6 -> 10, of which waited for: 6 -> 4; matrix products, arithmetic and copies ran while one was open for 3% -> 3% of each run, Pallas kernels for 0% -> 19%
where the time goes in v1:
time: 153 us
  Pallas kernels  50.2 us (33%)
  starting transfers between devices  31.5 us (21%)
  waiting for transfers between devices  26.2 us (17%)
  blocking collectives  24.7 us (16%)
  between operations  13.5 us (9%)
  local copies, waits for them, and re-layouts  3.37 us (2%)
  other arithmetic  3.3 us (2%)
    pallas_call x1, Pallas kernels, factor(): pl.pallas_call(factor_kernel, out_shape=[shape, shape], scratch_shapes=[p...  28.6 us
    pallas_call x1, Pallas kernels, update(): pl.pallas_call(update_kernel, grid_spec=pltpu.PrefetchScalarGridSpec(num_...  18.8 us
    ppermute x4, starting transfers between devices, shards(): lax.ppermute(turned[m], both, scatter_pairs(m))  16.4 us
    all_to_all x1, waiting for transfers between devices, shards(): d = lax.all_to_all(d, 'col', 0, 0, tiled=True)  15.8 us
    all_to_all x1, blocking collectives, shards(): lax.all_to_all(tile[0].reshape(16, 16, 256), 'col', 0, 0, tiled=True)[0:2]  14.3 us
    all_to_all x1, blocking collectives, shards(): d = lax.all_to_all(d, 'row', 0, 0, tiled=True)[0:2]  10.4 us
    ppermute x4, waiting for transfers between devices, shards(): lax.ppermute(turned[m], both, scatter_pairs(m))  8.04 us
    ppermute x3, starting transfers between devices, shards(): lax.ppermute(tile, 'row', [(k, 2 * z + k) for k in range(2)])  8.01 us
  transfers between devices with their start and end apart: 10, of which 4 were waited for; matrix products, arithmetic and copies ran while one was open for 3% of the time, Pallas kernels for 19%

profile of v1, /device:TPU:1, one launch (start us, length us, event | category | flops | bytes accessed | tf_op | source)
XLA Modules:
  0.0 152.7 jit_solution(5371650277790825456)
XLA Ops:
  6.5 0.0 all-gather.3.cloned.1.call-start
  6.5 2.8 %shard_map.17 = (f32[4,256,256]{2,1,0:T(8,128)}, f32[4,256,256]{2,1,0:T(8,128)}) custom-call(f32[16384,128]{1,0:T(8,128)} %bitcast.14), custom_call_target="tpu_custom_call" | custom-call | tf_op jit(solution)/shard_map/pallas_call | solution.py:43
  9.3 1.3 slice_bitcast_fusion.2
  10.6 6.0 %collective-permute-start.1 = (f32[256,256]{1,0:T(8,128)S(1)}, f32[256,256]{1,0:T(8,128)S(1)}, u32[]{:S(2)}, u32[]{:S(2)}) collective-permute-start(f32[256,256]{1,0:T(8,128)S(1)} %get-tuple-element.23), channel_id=1, source_target_pairs={{0,2},{1,19},{2,32},{3,49},{4,70},{5,87},{6,100},{7,117},{8,10},{9... | collective-permute-start | bytes 786440 | tf_op jit(solution)/shard_map/ppermute | solution.py:260
  16.6 7.0 %collective-permute-start.3 = (f32[256,256]{1,0:T(8,128)S(1)}, f32[256,256]{1,0:T(8,128)S(1)}, u32[]{:S(2)}, u32[]{:S(2)}) collective-permute-start(f32[256,256]{1,0:T(8,128)S(1)} %get-tuple-element.24), channel_id=1, source_target_pairs={{0,6},{1,23},{2,36},{3,53},{4,74},{5,91},{6,104},{7,121},{8,14},{9... | collective-permute-start | bytes 786440 | tf_op jit(solution)/shard_map/ppermute | solution.py:260
  23.7 1.3 collective-permute-start.2
  25.0 2.0 %collective-permute-start = (f32[256,256]{1,0:T(8,128)S(1)}, f32[256,256]{1,0:T(8,128)S(1)}, u32[]{:S(2)}, u32[]{:S(2)}) collective-permute-start(f32[256,256]{1,0:T(8,128)S(1)} %get-tuple-element.26), channel_id=1, source_target_pairs={{0,0},{1,17},{2,34},{3,51},{4,68},{5,85},{6,102},{7,119},{8,8},{9,... | collective-permute-start | bytes 786440 | tf_op jit(solution)/shard_map/ppermute | solution.py:260
  27.0 0.0 collective-permute-done.1
  27.0 2.4 %collective-permute-done.3 = f32[256,256]{1,0:T(8,128)S(1)} collective-permute-done((f32[256,256]{1,0:T(8,128)S(1)}, f32[256,256]{1,0:T(8,128)S(1)}, u32[]{:S(2)}, u32[]{:S(2)}) %collective-permute-start.3) | collective-permute-done | bytes 262176 | tf_op jit(solution)/shard_map/ppermute | solution.py:260
  29.4 5.6 %collective-permute-done.2 = f32[256,256]{1,0:T(8,128)S(1)} collective-permute-done((f32[256,256]{1,0:T(8,128)S(1)}, f32[256,256]{1,0:T(8,128)S(1)}, u32[]{:S(2)}, u32[]{:S(2)}) %collective-permute-start.2) | collective-permute-done | bytes 262176 | tf_op jit(solution)/shard_map/ppermute | solution.py:260
  35.0 0.0 collective-permute-done
  35.0 0.8 add_add_fusion
  35.8 0.0 all-gather.3.cloned.1.call-update
  35.8 1.0 slice.25
  36.8 14.3 %all_to_all.15 = f32[16,16,256]{2,1,0:T(8,128)S(1)} all-to-all(f32[16,16,256]{2,1,0:T(8,128)S(1)} %bitcast.18), channel_id=1, replica_groups=mesh['row'=8,'col'=16] {'col'}, dimensions={0} | all-to-all | bytes 524288 | tf_op jit(solution)/shard_map/all_to_all | solution.py:266
  51.1 10.4 %all_to_all.16 = f32[8,2,16,256]{3,2,1,0:T(8,128)S(1)} all-to-all(f32[8,2,16,256]{3,2,1,0:T(8,128)S(1)} %broadcast_in_dim.4), channel_id=1, replica_groups=mesh['row'=8,'col'=16] {'row'}, dimensions={0} | all-to-all | bytes 524288 | tf_op jit(solution)/shard_map/all_to_all | solution.py:268
  61.5 1.1 broadcast_in_dim.5
  62.6 3.9 %all-to-all-start.2 = ((f32[16,2,2,16,256]{4,3,2,1,0:T(8,128)}), f32[16,2,2,16,256]{4,3,2,1,0:T(8,128)S(1)}, u32[]{:S(2)}, u32[]{:S(2)}) async-start(f32[16,2,2,16,256]{4,3,2,1,0:T(8,128)} %broadcast_in_dim.5), calls=%async_computation.2 | async-start | bytes 2097152 | tf_op jit(solution)/shard_map/all_to_all | solution.py:270
  66.5 3.4 %collective-permute-start.6 = (f32[4,256,256]{2,1,0:T(8,128)}, f32[4,256,256]{2,1,0:T(8,128)}, u32[]{:S(2)}, u32[]{:S(2)}) collective-permute-start(f32[4,256,256]{2,1,0:T(8,128)} %get-tuple-element.15), channel_id=1, source_target_pairs={{0,64},{16,80},{1,65},{17,81},{2,66},{18,82},{3,67},{19,83},{4,68}... | collective-permute-start | bytes 3145736 | tf_op jit(solution)/shard_map/ppermute | solution.py:264
  69.9 2.3 %collective-permute-start.5 = (f32[4,256,256]{2,1,0:T(8,128)}, f32[4,256,256]{2,1,0:T(8,128)}, u32[]{:S(2)}, u32[]{:S(2)}) collective-permute-start(f32[4,256,256]{2,1,0:T(8,128)} %get-tuple-element.15), channel_id=1, source_target_pairs={{0,96},{16,112},{1,97},{17,113},{2,98},{18,114},{3,99},{19,115},{4... | collective-permute-start | bytes 3145736 | tf_op jit(solution)/shard_map/ppermute | solution.py:264
  72.2 2.3 %collective-permute-start.4 = (f32[4,256,256]{2,1,0:T(8,128)}, f32[4,256,256]{2,1,0:T(8,128)}, u32[]{:S(2)}, u32[]{:S(2)}) collective-permute-start(f32[4,256,256]{2,1,0:T(8,128)} %get-tuple-element.15), channel_id=1, source_target_pairs={{0,32},{16,48},{1,33},{17,49},{2,34},{18,50},{3,35},{19,51},{4,36}... | collective-permute-start | bytes 3145736 | tf_op jit(solution)/shard_map/ppermute | solution.py:264
  74.5 15.8 %all-to-all-done.2.d_ref = f32[16,2,2,16,256]{4,3,2,1,0:T(8,128)S(1)} async-done(((f32[16,2,2,16,256]{4,3,2,1,0:T(8,128)}), f32[16,2,2,16,256]{4,3,2,1,0:T(8,128)S(1)}, u32[]{:S(2)}, u32[]{:S(2)}) %all-to-all-start.2) | async-done | bytes 1048608 | tf_op jit(solution)/shard_map/all_to_all | solution.py:270
  90.3 28.6 %shard_map.18 = (f32[512,512]{1,0:T(8,128)S(1)}, f32[512,512]{1,0:T(8,128)S(1)}) custom-call(f32[16,2,2,16,256]{4,3,2,1,0:T(8,128)S(1)} %all-to-all-done.2.d_ref), custom_call_target="tpu_custom_call" | custom-call | flops 30000001024 | bytes 4194304 | tf_op jit(solution)/shard_map/pallas_call | solution.py:130
  118.9 0.0 collective-permute-done.6
  118.9 0.0 collective-permute-done.5
  118.9 0.0 collective-permute-done.4
  118.9 2.5 %add_select_fusion.mine_ref = f32[4,256,256]{2,1,0:T(8,128)S(1)} fusion(f32[4,256,256]{2,1,0:T(8,128)} %get-tuple-element.15, f32[4,256,256]{2,1,0:T(8,128)} %collective-permute-done.6, f32[4,256,256]{2,1,0:T(8,128)} %collective-permute-done.4, f32[4,256,256]{2,1,0:T(8,128)} %collective-permute-done.5, pred[]{:T(512)S(6)} %lt.3), kind=kLoop, calls=%fused_computation | loop fusion | flops 786432 | bytes 5242881 | tf_op jit(solution)/shard_map/jit(_where)/select_n | solution.py:274
  121.3 3.3 %collective-permute-start.7 = (f32[4,256,256]{2,1,0:T(8,128)S(1)}, f32[4,256,256]{2,1,0:T(8,128)}, u32[]{:S(2)}, u32[]{:S(2)}) collective-permute-start(f32[4,256,256]{2,1,0:T(8,128)S(1)} %add_select_fusion.mine_ref), channel_id=1, source_target_pairs={{0,16},{16,0},{32,48},{48,32},{64,80},{80,64},{96,112},{112,96},{1... | collective-permute-start | bytes 3145736 | tf_op jit(solution)/shard_map/ppermute | solution.py:275
  124.6 0.1 pad_add_fusion.place
  124.7 2.3 %collective-permute-done.7.other_ref = f32[4,256,256]{2,1,0:T(8,128)} collective-permute-done((f32[4,256,256]{2,1,0:T(8,128)S(1)}, f32[4,256,256]{2,1,0:T(8,128)}, u32[]{:S(2)}, u32[]{:S(2)}) %collective-permute-start.7) | collective-permute-done | bytes 1048608 | tf_op jit(solution)/shard_map/ppermute | solution.py:275
  127.0 0.0 all-gather.3.cloned.1.call-done
  127.0 18.8 %shard_map.19 = f32[16384,128]{1,0:T(8,128)} custom-call(s32[2]{0:T(128)S(1)} %pad_add_fusion.place, f32[16384,128]{1,0:T(8,128)} %bitcast.15, f32[16,256,256]{2,1,0:T(8,128)} %bitcast.16, f32[16,256,256]{2,1,0:T(8,128)} %bitcast.17, f32[512,512]{1,0:T(8,128)S(1)} %get-tuple-element.18.w_ref, f32[512,512]{1,0:T(8,128)S(1)} %get-tuple-element.19.lt_ref, ...), custom_call_target="tpu_custom_call" | custom-call | tf_op jit(solution)/shard_map/pallas_call | solution.py:222
  (3 shorter events, 0.0 us)
Async XLA Ops:
  6.5 120.5 %all-gather.3.cloned.1.call-start = ((), (), s32[]{:S(2)}) async-start(), calls=%async_computation.3 | async-start | bytes 4456448 | tf_op jit(solution)/shard_map/all_gather | solution.py:261
  10.6 16.4 %collective-permute-start.1 = (f32[256,256]{1,0:T(8,128)S(1)}, f32[256,256]{1,0:T(8,128)S(1)}, u32[]{:S(2)}, u32[]{:S(2)}) collective-permute-start(f32[256,256]{1,0:T(8,128)S(1)} %get-tuple-element.23), channel_id=1, source_target_pairs={{0,2},{1,19},{2,32},{3,49},{4,70},{5,87},{6,100},{7,117},{8,10},{9... | collective-permute-start | bytes 786440 | tf_op jit(solution)/shard_map/ppermute | solution.py:260
  16.6 12.8 %collective-permute-start.3 = (f32[256,256]{1,0:T(8,128)S(1)}, f32[256,256]{1,0:T(8,128)S(1)}, u32[]{:S(2)}, u32[]{:S(2)}) collective-permute-start(f32[256,256]{1,0:T(8,128)S(1)} %get-tuple-element.24), channel_id=1, source_target_pairs={{0,6},{1,23},{2,36},{3,53},{4,74},{5,91},{6,104},{7,121},{8,14},{9... | collective-permute-start | bytes 786440 | tf_op jit(solution)/shard_map/ppermute | solution.py:260
  23.7 11.4 %collective-permute-start.2 = (f32[256,256]{1,0:T(8,128)S(1)}, f32[256,256]{1,0:T(8,128)S(1)}, u32[]{:S(2)}, u32[]{:S(2)}) collective-permute-start(f32[256,256]{1,0:T(8,128)S(1)} %get-tuple-element.25), channel_id=1, source_target_pairs={{0,4},{1,21},{2,38},{3,55},{4,72},{5,89},{6,106},{7,123},{8,12},{9... | collective-permute-start | bytes 786440 | tf_op jit(solution)/shard_map/ppermute | solution.py:260
  25.0 10.1 %collective-permute-start = (f32[256,256]{1,0:T(8,128)S(1)}, f32[256,256]{1,0:T(8,128)S(1)}, u32[]{:S(2)}, u32[]{:S(2)}) collective-permute-start(f32[256,256]{1,0:T(8,128)S(1)} %get-tuple-element.26), channel_id=1, source_target_pairs={{0,0},{1,17},{2,34},{3,51},{4,68},{5,85},{6,102},{7,119},{8,8},{9,... | collective-permute-start | bytes 786440 | tf_op jit(solution)/shard_map/ppermute | solution.py:260
  62.6 27.7 %all-to-all-start.2 = ((f32[16,2,2,16,256]{4,3,2,1,0:T(8,128)}), f32[16,2,2,16,256]{4,3,2,1,0:T(8,128)S(1)}, u32[]{:S(2)}, u32[]{:S(2)}) async-start(f32[16,2,2,16,256]{4,3,2,1,0:T(8,128)} %broadcast_in_dim.5), calls=%async_computation.2 | async-start | bytes 2097152 | tf_op jit(solution)/shard_map/all_to_all | solution.py:270
  66.5 52.4 %collective-permute-start.6 = (f32[4,256,256]{2,1,0:T(8,128)}, f32[4,256,256]{2,1,0:T(8,128)}, u32[]{:S(2)}, u32[]{:S(2)}) collective-permute-start(f32[4,256,256]{2,1,0:T(8,128)} %get-tuple-element.15), channel_id=1, source_target_pairs={{0,64},{16,80},{1,65},{17,81},{2,66},{18,82},{3,67},{19,83},{4,68}... | collective-permute-start | bytes 3145736 | tf_op jit(solution)/shard_map/ppermute | solution.py:264
  69.9 49.0 %collective-permute-start.5 = (f32[4,256,256]{2,1,0:T(8,128)}, f32[4,256,256]{2,1,0:T(8,128)}, u32[]{:S(2)}, u32[]{:S(2)}) collective-permute-start(f32[4,256,256]{2,1,0:T(8,128)} %get-tuple-element.15), channel_id=1, source_target_pairs={{0,96},{16,112},{1,97},{17,113},{2,98},{18,114},{3,99},{19,115},{4... | collective-permute-start | bytes 3145736 | tf_op jit(solution)/shard_map/ppermute | solution.py:264
  72.2 46.7 %collective-permute-start.4 = (f32[4,256,256]{2,1,0:T(8,128)}, f32[4,256,256]{2,1,0:T(8,128)}, u32[]{:S(2)}, u32[]{:S(2)}) collective-permute-start(f32[4,256,256]{2,1,0:T(8,128)} %get-tuple-element.15), channel_id=1, source_target_pairs={{0,32},{16,48},{1,33},{17,49},{2,34},{18,50},{3,35},{19,51},{4,36}... | collective-permute-start | bytes 3145736 | tf_op jit(solution)/shard_map/ppermute | solution.py:264
  121.3 5.7 %collective-permute-start.7 = (f32[4,256,256]{2,1,0:T(8,128)S(1)}, f32[4,256,256]{2,1,0:T(8,128)}, u32[]{:S(2)}, u32[]{:S(2)}) collective-permute-start(f32[4,256,256]{2,1,0:T(8,128)S(1)} %add_select_fusion.mine_ref), channel_id=1, source_target_pairs={{0,16},{16,0},{32,48},{48,32},{64,80},{80,64},{96,112},{112,96},{1... | collective-permute-start | bytes 3145736 | tf_op jit(solution)/shard_map/ppermute | solution.py:275
Sparse Core Ops, SparseCore 0:
  36.0 62.0 all-gather.2

commit v2 on v1

v2 whole, which is shorter than its diff:
```python
import jax
import jax.numpy as jnp
from jax import lax
from jax.experimental import pallas as pl
from jax.experimental.pallas import tpu as pltpu
from jax.sharding import PartitionSpec as P

F32 = jnp.float32
BF16 = jnp.bfloat16
ROWS, COLS = 8, 16
MIB = 1024 * 1024


def dot(a, b, ca, cb):
    return lax.dot_general(
        a,
        b,
        (((ca,), (cb,)), ((), ())),
        precision=lax.Precision.HIGHEST,
        preferred_element_type=F32,
    )


def matmul(a, b):
    return jnp.dot(a, b, preferred_element_type=F32)


def split(x):
    high = x.astype(BF16)
    return high, (x - high.astype(F32)).astype(BF16)


def prepare_kernel(x_ref, tile_ref, tiles_ref, *rest):
    turned_refs, (rows, done) = rest[:4], rest[4:]
    copy = pltpu.make_async_copy(x_ref.at[0:2048], rows, done)
    copy.start()
    copy.wait()
    for m in range(4):
        for h in range(2):
            half = rows[pl.ds(2 * m + h, 256, stride=8), :]
            if m == 0:
                tile_ref[:, 128 * h : 128 * h + 128] = half
            tiles_ref[m, :, 128 * h : 128 * h + 128] = half
            turned_refs[m][128 * h : 128 * h + 128, :] = half.T


def prepare(x):
    vmem = pl.BlockSpec(memory_space=pltpu.VMEM)
    square = jax.ShapeDtypeStruct((256, 256), F32)
    return pl.pallas_call(
        prepare_kernel,
        in_specs=[pl.BlockSpec(memory_space=pl.ANY)],
        out_specs=[vmem] * 6,
        out_shape=[square, jax.ShapeDtypeStruct((4, 256, 256), F32)] + [square] * 4,
        scratch_shapes=[pltpu.VMEM((2048, 128), F32), pltpu.SemaphoreType.DMA],
        compiler_params=pltpu.CompilerParams(vmem_limit_bytes=58 * MIB),
    )(x)


def inner(block):
    n = 16
    rows = [block[8 * j : 8 * j + 8, :] for j in range(n)]
    lane = lax.broadcasted_iota(jnp.int32, (8, 128), 1)
    sub = lax.broadcasted_iota(jnp.int32, (8, 128), 0)
    inv_rows = [jnp.where(lane == sub + 8 * j, 1.0, 0.0).astype(jnp.float32) for j in range(n)]
    full = lambda v: jnp.broadcast_to(v, (8, 128))
    us, ws = [], []
    for j in range(n):
        r, e = rows[j], inv_rows[j]
        cols = [full(r[:, 8 * j + c : 8 * j + c + 1]) for c in range(8)]
        a = [[full(cols[c][i : i + 1, :]) if i >= c else None for c in range(8)] for i in range(8)]
        l = [[None] * 8 for _ in range(8)]
        inv = [None] * 8
        for c in range(8):
            inv[c] = lax.rsqrt(a[c][c])
            for i in range(c + 1, 8):
                l[i][c] = a[i][c] * inv[c]
            for d in range(c + 1, 8):
                for i in range(d, 8):
                    a[i][d] = a[i][d] - l[i][c] * l[d][c]
        ru = [full(r[i : i + 1, :]) for i in range(8)]
        eu = [full(e[i : i + 1, :]) for i in range(8)]
        for c in range(8):
            ru[c] = ru[c] * inv[c]
            eu[c] = eu[c] * inv[c]
            for i in range(c + 1, 8):
                ru[i] = ru[i] - l[i][c] * ru[c]
                eu[i] = eu[i] - l[i][c] * eu[c]
        u, w = ru[0], eu[0]
        for c in range(1, 8):
            u = jnp.where(sub == c, ru[c], u)
            w = jnp.where(sub == c, eu[c], w)
        us.append(u)
        ws.append(w)
        for i in range(j + 1, n):
            ri, ei = rows[i], inv_rows[i]
            v = [full(ri[:, 8 * j + c : 8 * j + c + 1]) for c in range(8)]
            for c in range(8):
                v[c] = v[c] * inv[c]
                for d in range(c + 1, 8):
                    v[d] = v[d] - l[d][c] * v[c]
            for c in range(8):
                ri = ri - v[c] * ru[c]
                ei = ei - v[c] * eu[c]
            rows[i], inv_rows[i] = ri, ei
    return jnp.concatenate(us, axis=0), jnp.concatenate(ws, axis=0)

def factor_256(s, lt_ref, w_ref, diag):
    r1 = lax.broadcasted_iota(jnp.int32, (128, 128), 0)
    c1 = lax.broadcasted_iota(jnp.int32, (128, 128), 1)
    right = s[0:128, 128:256]
    diag[0] = s[0:128, 0:128]
    diag[1] = s[128:256, 128:256]
    lt_ref[128:256, 0:128] = jnp.zeros((128, 128), F32)
    w_ref[0:128, 128:256] = jnp.zeros((128, 128), F32)

    @pl.loop(0, 2)
    def _(k):
        at = pl.multiple_of(k * 128, 128)
        u, w = inner(diag[k])
        w = jnp.where(c1 <= r1, w, 0.0)
        lt_ref[pl.ds(at, 128), pl.ds(at, 128)] = jnp.where(c1 >= r1, u, 0.0)
        w_ref[pl.ds(at, 128), pl.ds(at, 128)] = w

        @pl.when(k == 0)
        def _():
            u01 = dot(w, right, 1, 0)
            lt_ref[0:128, 128:256] = u01
            diag[1] -= dot(u01, u01, 0, 0)

    under = dot(lt_ref[0:128, 128:256], w_ref[0:128, 0:128], 0, 0)
    w_ref[128:256, 0:128] = -dot(w_ref[128:256, 128:256], under, 1, 0)


def factor_kernel(d_ref, *rest):
    lt0_ref, lt1_ref, w0_ref, w1_ref, under_ref, s, right, diag = rest
    for j in range(16):
        at = slice(16 * j, 16 * j + 16)
        s[at, :] = d_ref[j, 0]
    factor_256(s, lt0_ref, w0_ref, diag)
    for j in range(16):
        at = slice(16 * j, 16 * j + 16)
        right[at, :] = d_ref[j, 1]
        s[at, :] = d_ref[j, 2]
    u = dot(w0_ref[...], right[...], 1, 0)
    s[...] -= dot(u, u, 0, 0)
    factor_256(s, lt1_ref, w1_ref, diag)
    under_ref[...] = -dot(w1_ref[...], dot(u, w0_ref[...], 0, 0), 1, 0)


def factor(d):
    square = jax.ShapeDtypeStruct((256, 256), F32)
    return pl.pallas_call(
        factor_kernel,
        out_shape=[square] * 5,
        scratch_shapes=[pltpu.VMEM((256, 256), F32)] * 2 + [pltpu.VMEM((2, 128, 128), F32)],
        compiler_params=pltpu.CompilerParams(vmem_limit_bytes=16 * MIB),
        cost_estimate=pl.CostEstimate(flops=0, bytes_accessed=0, transcendentals=0),
    )(d)


def update_kernel(
    place, x_ref, g_ref, w0_ref, w1_ref, under_ref, lt0_ref, lt1_ref, mine_ref, other_ref, out_ref,
    old, new, tiles, wt, bc, old_sem, new_sem, tile_sem,
):
    row, col = place[0], place[1]

    def load(l, mh):
        at = pl.ds(l * 256, 256)
        return pltpu.make_async_copy(
            x_ref.at[at, mh], old.at[l, :, pl.ds(128 * mh, 128)], old_sem.at[l, mh]
        )

    def fetch(l, k):
        return pltpu.make_async_copy(
            g_ref.at[position(row, l, k)], tiles.at[l, k], tile_sem.at[l, k]
        )

    def store(l, mh):
        at = pl.ds(l * 256, 256)
        return pltpu.make_async_copy(
            new.at[l % 2, :, pl.ds(128 * mh, 128)], out_ref.at[at, mh], new_sem.at[l % 2, mh]
        )

    @pl.loop(0, 8)
    def _(l):
        for k in range(2):
            fetch(l, k).start()
        for mh in range(8):
            load(l, mh).start()

    w = jnp.concatenate(
        [
            jnp.concatenate([w0_ref[...], jnp.zeros((256, 256), F32)], axis=1),
            jnp.concatenate([under_ref[...], w1_ref[...]], axis=1),
        ],
        axis=0,
    )
    high, low = split(w.T)
    wt[0:512, :] = high
    wt[512:1024, :] = low
    high, low = split(w)
    is_first = lax.rem(row, 2) == 0
    for m in range(4):
        mine, other = mine_ref[m], other_ref[m]
        a0h, a0l = split(jnp.where(is_first, mine, other))
        a1h, a1l = split(jnp.where(is_first, other, mine))
        b0 = matmul(high[0:256, 0:256], a0h) + (
            matmul(high[0:256, 0:256], a0l) + matmul(low[0:256, 0:256], a0h)
        )
        ah = jnp.concatenate([a0h, a1h], axis=0)
        al = jnp.concatenate([a0l, a1l], axis=0)
        b1 = matmul(high[256:512], ah) + (matmul(high[256:512], al) + matmul(low[256:512], ah))
        bh, bl = split(jnp.concatenate([b0, b1], axis=0))
        bc[0:512, 256 * m : 256 * m + 256] = bh
        bc[512:1024, 256 * m : 256 * m + 256] = bl
        bc[1024:1536, 256 * m : 256 * m + 256] = bh

    @pl.loop(0, 8)
    def _(l):
        for k in range(2):
            fetch(l, k).wait()
        x0h, x0l = split(tiles[l, 0])
        x1h, x1l = split(tiles[l, 1])
        wh, wl = wt[0:512, :], wt[512:1024, :]
        b0 = matmul(x0h, wh[0:256, 0:256]) + (
            matmul(x0l, wh[0:256, 0:256]) + matmul(x0h, wl[0:256, 0:256])
        )
        xh = jnp.concatenate([x0h, x1h], axis=1)
        xl = jnp.concatenate([x0l, x1l], axis=1)
        b1 = matmul(xh, wh[:, 256:512]) + (
            matmul(xl, wh[:, 256:512]) + matmul(xh, wl[:, 256:512])
        )
        bh, bl = split(jnp.concatenate([b0, b1], axis=1))
        left = jnp.concatenate([bh, bh, bl], axis=1)

        for mh in range(8):
            load(l, mh).wait()

        @pl.when(l >= 2)
        def _():
            for mh in range(8):
                store(l - 2, mh).wait()

        slot = l % 2
        for m in range(4):
            at = slice(256 * m, 256 * m + 256)
            new[slot, :, at] = old[l, :, at] - matmul(left, bc[:, at])

        @pl.when(col <= 1)
        def _():
            new[slot, :, 0:256] = jnp.where(col == 0, b0, b1)

        @pl.when((l == 0) & (row <= 1))
        def _():
            zero = jnp.zeros((256, 256), F32)
            new[slot, :, 256:1024] = jnp.zeros((256, 768), F32)
            new[slot, :, 0:256] = jnp.where(
                row == 0,
                jnp.where(col == 0, lt0_ref[...].T, zero),
                jnp.where(col == 0, b0, jnp.where(col == 1, lt1_ref[...].T, zero)),
            )

        for mh in range(8):
            store(l, mh).start()

    for l in (6, 7):
        for mh in range(8):
            store(l, mh).wait()


def position(row, l, k):
    q = 2 * (l // 2) + k
    x = (row // 4 + 2 * (l % 2) + q // 4) % 4
    y = (row % 4 + q % 4) % 4
    return 4 * x + y


def update(place, x, gathered, w0, w1, under, lt0, lt1, mine, other):
    vmem = pl.BlockSpec(memory_space=pltpu.VMEM)
    hbm = pl.BlockSpec(memory_space=pl.ANY)
    return pl.pallas_call(
        update_kernel,
        in_specs=[pl.BlockSpec(memory_space=pltpu.SMEM), hbm, hbm] + [vmem] * 7,
        out_specs=hbm,
        out_shape=jax.ShapeDtypeStruct((2048, 8, 128), F32),
        scratch_shapes=[
            pltpu.VMEM((8, 256, 1024), F32),
            pltpu.VMEM((2, 256, 1024), F32),
            pltpu.VMEM((8, 2, 256, 256), F32),
            pltpu.VMEM((1024, 512), BF16),
            pltpu.VMEM((1536, 1024), BF16),
            pltpu.SemaphoreType.DMA((8, 8)),
            pltpu.SemaphoreType.DMA((2, 8)),
            pltpu.SemaphoreType.DMA((8, 2)),
        ],
        compiler_params=pltpu.CompilerParams(vmem_limit_bytes=48 * MIB),
    )(place, x, gathered, w0, w1, under, lt0, lt1, mine, other)


def scatter_pairs(m):
    pairs = []
    for k in range(2):
        for c in range(COLS):
            row = c % ROWS
            target = position(row, 2 * m + c // ROWS, k)
            pairs.append((k * COLS + c, row * COLS + target))
    return pairs


def along_z(array, step):
    return lax.ppermute(array, "row", [(k, 2 * step + k) for k in range(2)])


def shards(kernel):
    row, col = lax.axis_index("row"), lax.axis_index("col")
    place = jnp.stack([row, col]).astype(jnp.int32)
    x = kernel.reshape(16384, 128)
    tile, tiles, *turned = prepare(x)

    pieces = [lax.ppermute(turned[m], ("row", "col"), scatter_pairs(m)) for m in range(4)]
    d = lax.all_to_all(tile.reshape(16, 16, 256), "col", 0, 0, tiled=True)[0:2]
    pieces, d = lax.optimization_barrier((pieces, d))
    share = sum(pieces)
    share, d = lax.optimization_barrier((share, d))
    gathered = lax.all_gather(share, "col")

    d = lax.all_to_all(jnp.broadcast_to(d[None], (8, 2, 16, 256)), "row", 0, 0, tiled=True)
    d = jnp.stack([d[0, 0], d[0, 1], d[1, 1]])
    tiles, d = lax.optimization_barrier((tiles, d))
    came = [along_z(tiles, step) for step in (1, 3, 2)]
    d = lax.all_to_all(jnp.broadcast_to(d[None], (16, 3, 16, 256)), "col", 0, 0, tiled=True)
    lt0, lt1, w0, w1, under = factor(d)

    came, w1 = lax.optimization_barrier((came, w1))
    mine = jnp.where(row < 2, tiles, sum(came))
    other = lax.ppermute(mine, "row", [(r, r ^ 1) for r in range(ROWS)])
    cells = kernel.reshape(2048, 8, 128)
    out = update(place, cells, gathered, w0, w1, under, lt0, lt1, mine, other)
    return out.reshape(kernel.shape)


def solution(mesh):
    placed = P(None, "row", None, None, "col", None)
    return jax.shard_map(
        shards, mesh=mesh, in_specs=(placed,), out_specs=placed, check_vma=False
    )
```

time: 153 us -> 129 us (0.84)
  Pallas kernels: 50.2 us -> 39.9 us
  waiting for transfers between devices: 26.2 us -> 17.6 us
  starting transfers between devices: 31.5 us -> 27.9 us
  local copies, waits for them, and re-layouts: 3.37 us -> 1.02 us
    pallas_call x3, Pallas kernels: 50.2 us -> 39.9 us  [the longest x1 19.8 us: factor(): pl.pallas_call(factor_kernel, out_shape=[square] * 5, scratch_shapes=[plt...]
    ppermute x7, waiting for transfers between devices: 8.05 us -> 2.62 us  [the longest x3 2.61 us: along_z(): return lax.ppermute(array, 'row', [(k, 2 * step + k) for k in range(2)])]
    all_to_all x1, waiting for transfers between devices: 15.8 us -> 12.8 us  [shards(): lax.all_to_all(jnp.broadcast_to(d[None], (16, 3, 16, 256)), 'col', 0, 0,...]
    ppermute x7, starting transfers between devices: 24.4 us -> 22.4 us  [the longest x4 15 us: shards(): lax.ppermute(turned[m], ('row', 'col'), scatter_pairs(m))]
    ppermute x1, starting transfers between devices: 3.28 us -> 1.49 us  [shards(): other = lax.ppermute(mine, 'row', [(r, r ^ 1) for r in range(ROWS)])]
  transfers between devices with their start and end apart: 10 -> 10, of which waited for: 4 -> 3; matrix products, arithmetic and copies ran while one was open for 3% -> 3% of each run, Pallas kernels for 19% -> 15%
where the time goes in v2:
time: 129 us
  Pallas kernels  39.9 us (31%)
  starting transfers between devices  27.9 us (22%)
  blocking collectives  25.8 us (20%)
  waiting for transfers between devices  17.6 us (14%)
  between operations  13.5 us (10%)
  other arithmetic  2.98 us (2%)
    pallas_call x1, Pallas kernels, factor(): pl.pallas_call(factor_kernel, out_shape=[square] * 5, scratch_shapes=[plt...  19.8 us
    all_to_all x1, blocking collectives, shards(): d = lax.all_to_all(tile.reshape(16, 16, 256), 'col', 0, 0, tiled=True)[0:2]  17.2 us
    pallas_call x1, Pallas kernels, update(): pl.pallas_call(update_kernel, in_specs=[pl.BlockSpec(memory_space=pltpu.S...  17.2 us
    ppermute x4, starting transfers between devices, shards(): lax.ppermute(turned[m], ('row', 'col'), scatter_pairs(m))  15 us
    all_to_all x1, waiting for transfers between devices, shards(): lax.all_to_all(jnp.broadcast_to(d[None], (16, 3, 16, 256)), 'col', 0, 0,...  12.8 us
    all_to_all x1, blocking collectives, shards(): lax.all_to_all(jnp.broadcast_to(d[None], (8, 2, 16, 256)), 'row', 0, 0, t...  8.57 us
    ppermute x3, starting transfers between devices, along_z(): return lax.ppermute(array, 'row', [(k, 2 * step + k) for k in range(2)])  7.34 us
    all_to_all x1, starting transfers between devices, shards(): lax.all_to_all(jnp.broadcast_to(d[None], (16, 3, 16, 256)), 'col', 0, 0,...  4.01 us
  transfers between devices with their start and end apart: 10, of which 3 were waited for; matrix products, arithmetic and copies ran while one was open for 3% of the time, Pallas kernels for 15%

profile of v2, /device:TPU:1, one launch (start us, length us, event | category | flops | bytes accessed | tf_op | source)
XLA Modules:
  0.0 128.7 jit_solution(6725614340855023340)
XLA Ops:
  6.5 0.0 all-gather.3.cloned.1.call-start
  6.5 2.8 %shard_map.17 = (f32[256,256]{1,0:T(8,128)}, f32[4,256,256]{2,1,0:T(8,128)}, f32[256,256]{1,0:T(8,128)}, f32[256,256]{1,0:T(8,128)}, f32[256,256]{1,0:T(8,128)}, /*index=5*/f32[256,256]{1,0:T(8,128)}) custom-call(f32[16384,128]{1,0:T(8,128)} %bitcast.13), custom_call_target="tpu_custom_call" | custom-call | tf_op jit(solution)/shard_map/pallas_call | solution.py:50
  9.3 4.6 %collective-permute-start = (f32[256,256]{1,0:T(8,128)}, f32[256,256]{1,0:T(8,128)S(1)}, u32[]{:S(2)}, u32[]{:S(2)}) collective-permute-start(f32[256,256]{1,0:T(8,128)} %get-tuple-element.29), channel_id=1, source_target_pairs={{0,0},{1,17},{2,34},{3,51},{4,68},{5,85},{6,102},{7,119},{8,8},{9,... | collective-permute-start | bytes 786440 | tf_op jit(solution)/shard_map/ppermute | solution.py:321
  14.0 4.7 %collective-permute-start.1 = (f32[256,256]{1,0:T(8,128)}, f32[256,256]{1,0:T(8,128)S(1)}, u32[]{:S(2)}, u32[]{:S(2)}) collective-permute-start(f32[256,256]{1,0:T(8,128)} %get-tuple-element.30), channel_id=1, source_target_pairs={{0,2},{1,19},{2,32},{3,49},{4,70},{5,87},{6,100},{7,117},{8,10},{9... | collective-permute-start | bytes 786440 | tf_op jit(solution)/shard_map/ppermute | solution.py:321
  18.7 3.9 %collective-permute-start.2 = (f32[256,256]{1,0:T(8,128)}, f32[256,256]{1,0:T(8,128)S(1)}, u32[]{:S(2)}, u32[]{:S(2)}) collective-permute-start(f32[256,256]{1,0:T(8,128)} %get-tuple-element.31), channel_id=1, source_target_pairs={{0,4},{1,21},{2,38},{3,55},{4,72},{5,89},{6,106},{7,123},{8,12},{9... | collective-permute-start | bytes 786440 | tf_op jit(solution)/shard_map/ppermute | solution.py:321
  22.5 1.8 %collective-permute-start.3 = (f32[256,256]{1,0:T(8,128)}, f32[256,256]{1,0:T(8,128)S(1)}, u32[]{:S(2)}, u32[]{:S(2)}) collective-permute-start(f32[256,256]{1,0:T(8,128)} %get-tuple-element.32), channel_id=1, source_target_pairs={{0,6},{1,23},{2,36},{3,53},{4,74},{5,91},{6,104},{7,121},{8,14},{9... | collective-permute-start | bytes 786440 | tf_op jit(solution)/shard_map/ppermute | solution.py:321
  24.4 17.2 %all_to_all.15 = f32[16,16,256]{2,1,0:T(8,128)S(1)} all-to-all(f32[16,16,256]{2,1,0:T(8,128)} %bitcast.16), channel_id=1, replica_groups=mesh['row'=8,'col'=16] {'col'}, dimensions={0} | all-to-all | bytes 524288 | tf_op jit(solution)/shard_map/all_to_all | solution.py:322
  41.6 0.0 collective-permute-done
  41.6 0.0 collective-permute-done.1
  41.7 0.0 collective-permute-done.2
  41.7 0.0 collective-permute-done.3
  41.7 0.8 add_add_fusion
  42.4 0.0 all-gather.3.cloned.1.call-update
  42.5 8.6 %all_to_all.16 = f32[8,2,16,256]{3,2,1,0:T(8,128)S(1)} all-to-all(f32[8,2,16,256]{3,2,1,0:T(8,128)S(1)} %broadcast_in_dim.4), channel_id=1, replica_groups=mesh['row'=8,'col'=16] {'row'}, dimensions={0} | all-to-all | bytes 524288 | tf_op jit(solution)/shard_map/all_to_all | solution.py:328
  51.1 2.8 %collective-permute-start.6 = (f32[4,256,256]{2,1,0:T(8,128)}, f32[4,256,256]{2,1,0:T(8,128)S(1)}, u32[]{:S(2)}, u32[]{:S(2)}) collective-permute-start(f32[4,256,256]{2,1,0:T(8,128)} %get-tuple-element.44), channel_id=1, source_target_pairs={{0,64},{16,80},{1,65},{17,81},{2,66},{18,82},{3,67},{19,83},{4,68}... | collective-permute-start | bytes 3145736 | tf_op jit(solution)/shard_map/ppermute | solution.py:312
  53.9 2.3 %collective-permute-start.5 = (f32[4,256,256]{2,1,0:T(8,128)}, f32[4,256,256]{2,1,0:T(8,128)}, u32[]{:S(2)}, u32[]{:S(2)}) collective-permute-start(f32[4,256,256]{2,1,0:T(8,128)} %get-tuple-element.44), channel_id=1, source_target_pairs={{0,96},{16,112},{1,97},{17,113},{2,98},{18,114},{3,99},{19,115},{4... | collective-permute-start | bytes 3145736 | tf_op jit(solution)/shard_map/ppermute | solution.py:312
  56.2 2.3 %collective-permute-start.4 = (f32[4,256,256]{2,1,0:T(8,128)}, f32[4,256,256]{2,1,0:T(8,128)}, u32[]{:S(2)}, u32[]{:S(2)}) collective-permute-start(f32[4,256,256]{2,1,0:T(8,128)} %get-tuple-element.44), channel_id=1, source_target_pairs={{0,32},{16,48},{1,33},{17,49},{2,34},{18,50},{3,35},{19,51},{4,36}... | collective-permute-start | bytes 3145736 | tf_op jit(solution)/shard_map/ppermute | solution.py:312
  58.4 1.0 broadcast_in_dim.5
  59.4 4.0 %all-to-all-start.2 = ((f32[16,3,16,256]{3,2,1,0:T(8,128)}), f32[16,3,16,256]{3,2,1,0:T(8,128)S(1)}, u32[]{:S(2)}, u32[]{:S(2)}) async-start(f32[16,3,16,256]{3,2,1,0:T(8,128)} %broadcast_in_dim.5), calls=%async_computation.2 | async-start | bytes 1572864 | tf_op jit(solution)/shard_map/all_to_all | solution.py:332
  63.5 12.8 %all-to-all-done.2.d_ref = f32[16,3,16,256]{3,2,1,0:T(8,128)S(1)} async-done(((f32[16,3,16,256]{3,2,1,0:T(8,128)}), f32[16,3,16,256]{3,2,1,0:T(8,128)S(1)}, u32[]{:S(2)}, u32[]{:S(2)}) %all-to-all-start.2) | async-done | bytes 786464 | tf_op jit(solution)/shard_map/all_to_all | solution.py:332
  76.2 19.8 %shard_map.18 = (f32[256,256]{1,0:T(8,128)S(1)}, f32[256,256]{1,0:T(8,128)S(1)}, f32[256,256]{1,0:T(8,128)S(1)}, f32[256,256]{1,0:T(8,128)S(1)}, f32[256,256]{1,0:T(8,128)S(1)}) custom-call(f32[16,3,16,256]{3,2,1,0:T(8,128)S(1)} %all-to-all-done.2.d_ref), custom_call_target="tpu_custom_call" | custom-call | tf_op jit(solution)/shard_map/pallas_call | solution.py:153
  96.1 0.0 collective-permute-done.6
  96.1 0.0 collective-permute-done.5
  96.1 2.6 %collective-permute-done.4 = f32[4,256,256]{2,1,0:T(8,128)} collective-permute-done((f32[4,256,256]{2,1,0:T(8,128)}, f32[4,256,256]{2,1,0:T(8,128)}, u32[]{:S(2)}, u32[]{:S(2)}) %collective-permute-start.4) | collective-permute-done | bytes 1048608 | tf_op jit(solution)/shard_map/ppermute | solution.py:312
  98.7 2.1 %add_select_fusion.mine_ref = f32[4,256,256]{2,1,0:T(8,128)S(1)} fusion(f32[4,256,256]{2,1,0:T(8,128)} %get-tuple-element.44, f32[4,256,256]{2,1,0:T(8,128)S(1)} %collective-permute-done.6, f32[4,256,256]{2,1,0:T(8,128)} %collective-permute-done.4, f32[4,256,256]{2,1,0:T(8,128)} %collective-permute-done.5, pred[]{:T(512)S(6)} %lt.3), kind=kLoop, calls=%fused_computation | loop fusion | flops 786432 | bytes 5242881 | tf_op jit(solution)/shard_map/jit(_where)/select_n | solution.py:336
  100.8 1.5 %collective-permute-start.7 = (f32[4,256,256]{2,1,0:T(8,128)S(1)}, f32[4,256,256]{2,1,0:T(8,128)S(1)}, u32[]{:S(2)}, u32[]{:S(2)}) collective-permute-start(f32[4,256,256]{2,1,0:T(8,128)S(1)} %add_select_fusion.mine_ref), channel_id=1, source_target_pairs={{0,16},{16,0},{32,48},{48,32},{64,80},{80,64},{96,112},{112,96},{1... | collective-permute-start | bytes 3145736 | tf_op jit(solution)/shard_map/ppermute | solution.py:337
  102.3 0.1 pad_add_fusion.place
  102.4 2.2 %collective-permute-done.7.other_ref = f32[4,256,256]{2,1,0:T(8,128)S(1)} collective-permute-done((f32[4,256,256]{2,1,0:T(8,128)S(1)}, f32[4,256,256]{2,1,0:T(8,128)S(1)}, u32[]{:S(2)}, u32[]{:S(2)}) %collective-permute-start.7) | collective-permute-done | bytes 1048608 | tf_op jit(solution)/shard_map/ppermute | solution.py:337
  104.6 0.0 all-gather.3.cloned.1.call-done
  104.6 17.2 %shard_map.19 = f32[2048,8,128]{2,1,0:T(8,128)} custom-call(s32[2]{0:T(128)S(1)} %pad_add_fusion.place, f32[2048,8,128]{2,1,0:T(8,128)} %bitcast.14, f32[16,256,256]{2,1,0:T(8,128)} %bitcast.15, f32[256,256]{1,0:T(8,128)S(1)} %get-tuple-element.43.w0_ref, f32[256,256]{1,0:T(8,128)S(1)} %get-tuple-element.46.w1_ref, ...), custom_call_target="tpu_custom_call" | custom-call | tf_op jit(solution)/shard_map/pallas_call | solution.py:282
  (4 shorter events, 0.0 us)
Async XLA Ops:
  6.5 98.1 %all-gather.3.cloned.1.call-start = ((), (), s32[]{:S(2)}) async-start(), calls=%async_computation.3 | async-start | bytes 4456448 | tf_op jit(solution)/shard_map/all_gather | solution.py:326
  9.3 32.3 %collective-permute-start = (f32[256,256]{1,0:T(8,128)}, f32[256,256]{1,0:T(8,128)S(1)}, u32[]{:S(2)}, u32[]{:S(2)}) collective-permute-start(f32[256,256]{1,0:T(8,128)} %get-tuple-element.29), channel_id=1, source_target_pairs={{0,0},{1,17},{2,34},{3,51},{4,68},{5,85},{6,102},{7,119},{8,8},{9,... | collective-permute-start | bytes 786440 | tf_op jit(solution)/shard_map/ppermute | solution.py:321
  14.0 27.7 %collective-permute-start.1 = (f32[256,256]{1,0:T(8,128)}, f32[256,256]{1,0:T(8,128)S(1)}, u32[]{:S(2)}, u32[]{:S(2)}) collective-permute-start(f32[256,256]{1,0:T(8,128)} %get-tuple-element.30), channel_id=1, source_target_pairs={{0,2},{1,19},{2,32},{3,49},{4,70},{5,87},{6,100},{7,117},{8,10},{9... | collective-permute-start | bytes 786440 | tf_op jit(solution)/shard_map/ppermute | solution.py:321
  18.7 23.0 %collective-permute-start.2 = (f32[256,256]{1,0:T(8,128)}, f32[256,256]{1,0:T(8,128)S(1)}, u32[]{:S(2)}, u32[]{:S(2)}) collective-permute-start(f32[256,256]{1,0:T(8,128)} %get-tuple-element.31), channel_id=1, source_target_pairs={{0,4},{1,21},{2,38},{3,55},{4,72},{5,89},{6,106},{7,123},{8,12},{9... | collective-permute-start | bytes 786440 | tf_op jit(solution)/shard_map/ppermute | solution.py:321
  22.5 19.1 %collective-permute-start.3 = (f32[256,256]{1,0:T(8,128)}, f32[256,256]{1,0:T(8,128)S(1)}, u32[]{:S(2)}, u32[]{:S(2)}) collective-permute-start(f32[256,256]{1,0:T(8,128)} %get-tuple-element.32), channel_id=1, source_target_pairs={{0,6},{1,23},{2,36},{3,53},{4,74},{5,91},{6,104},{7,121},{8,14},{9... | collective-permute-start | bytes 786440 | tf_op jit(solution)/shard_map/ppermute | solution.py:321
  51.1 45.0 %collective-permute-start.6 = (f32[4,256,256]{2,1,0:T(8,128)}, f32[4,256,256]{2,1,0:T(8,128)S(1)}, u32[]{:S(2)}, u32[]{:S(2)}) collective-permute-start(f32[4,256,256]{2,1,0:T(8,128)} %get-tuple-element.44), channel_id=1, source_target_pairs={{0,64},{16,80},{1,65},{17,81},{2,66},{18,82},{3,67},{19,83},{4,68}... | collective-permute-start | bytes 3145736 | tf_op jit(solution)/shard_map/ppermute | solution.py:312
  53.9 42.2 %collective-permute-start.5 = (f32[4,256,256]{2,1,0:T(8,128)}, f32[4,256,256]{2,1,0:T(8,128)}, u32[]{:S(2)}, u32[]{:S(2)}) collective-permute-start(f32[4,256,256]{2,1,0:T(8,128)} %get-tuple-element.44), channel_id=1, source_target_pairs={{0,96},{16,112},{1,97},{17,113},{2,98},{18,114},{3,99},{19,115},{4... | collective-permute-start | bytes 3145736 | tf_op jit(solution)/shard_map/ppermute | solution.py:312
  56.2 42.5 %collective-permute-start.4 = (f32[4,256,256]{2,1,0:T(8,128)}, f32[4,256,256]{2,1,0:T(8,128)}, u32[]{:S(2)}, u32[]{:S(2)}) collective-permute-start(f32[4,256,256]{2,1,0:T(8,128)} %get-tuple-element.44), channel_id=1, source_target_pairs={{0,32},{16,48},{1,33},{17,49},{2,34},{18,50},{3,35},{19,51},{4,36}... | collective-permute-start | bytes 3145736 | tf_op jit(solution)/shard_map/ppermute | solution.py:312
  59.4 16.8 %all-to-all-start.2 = ((f32[16,3,16,256]{3,2,1,0:T(8,128)}), f32[16,3,16,256]{3,2,1,0:T(8,128)S(1)}, u32[]{:S(2)}, u32[]{:S(2)}) async-start(f32[16,3,16,256]{3,2,1,0:T(8,128)} %broadcast_in_dim.5), calls=%async_computation.2 | async-start | bytes 1572864 | tf_op jit(solution)/shard_map/all_to_all | solution.py:332
  100.8 3.8 %collective-permute-start.7 = (f32[4,256,256]{2,1,0:T(8,128)S(1)}, f32[4,256,256]{2,1,0:T(8,128)S(1)}, u32[]{:S(2)}, u32[]{:S(2)}) collective-permute-start(f32[4,256,256]{2,1,0:T(8,128)S(1)} %add_select_fusion.mine_ref), channel_id=1, source_target_pairs={{0,16},{16,0},{32,48},{48,32},{64,80},{80,64},{96,112},{112,96},{1... | collective-permute-start | bytes 3145736 | tf_op jit(solution)/shard_map/ppermute | solution.py:337
Sparse Core Ops, SparseCore 0:
  42.6 52.1 all-gather.2

commit v3 on v2

--- a/solution.py
+++ b/solution.py
@@ -159,36 +159,11 @@
     )(d)
 
 
-def update_kernel(
-    place, x_ref, g_ref, w0_ref, w1_ref, under_ref, lt0_ref, lt1_ref, mine_ref, other_ref, out_ref,
-    old, new, tiles, wt, bc, old_sem, new_sem, tile_sem,
-):
-    row, col = place[0], place[1]
-
-    def load(l, mh):
-        at = pl.ds(l * 256, 256)
-        return pltpu.make_async_copy(
-            x_ref.at[at, mh], old.at[l, :, pl.ds(128 * mh, 128)], old_sem.at[l, mh]
-        )
-
-    def fetch(l, k):
-        return pltpu.make_async_copy(
-            g_ref.at[position(row, l, k)], tiles.at[l, k], tile_sem.at[l, k]
-        )
-
-    def store(l, mh):
-        at = pl.ds(l * 256, 256)
-        return pltpu.make_async_copy(
-            new.at[l % 2, :, pl.ds(128 * mh, 128)], out_ref.at[at, mh], new_sem.at[l % 2, mh]
-        )
-
-    @pl.loop(0, 8)
-    def _(l):
-        for k in range(2):
-            fetch(l, k).start()
-        for mh in range(8):
-            load(l, mh).start()
-
+def product(a, b):
+    return matmul(a[0], b[0]) + (matmul(a[0], b[1]) + matmul(a[1], b[0]))
+
+
+def columns(is_first, w0_ref, w1_ref, under_ref, column, wt_ref, z_ref):
     w = jnp.concatenate(
         [
             jnp.concatenate([w0_ref[...], jnp.zeros((256, 256), F32)], axis=1),
@@ -196,43 +171,77 @@
         ],
         axis=0,
     )
-    high, low = split(w.T)
-    wt[0:512, :] = high
-    wt[512:1024, :] = low
-    high, low = split(w)
-    is_first = lax.rem(row, 2) == 0
+    turned = split(w.T)
+    wt_ref[0:512, :] = turned[0]
+    wt_ref[512:1024, :] = turned[1]
+    w = split(w)
     for m in range(4):
-        mine, other = mine_ref[m], other_ref[m]
-        a0h, a0l = split(jnp.where(is_first, mine, other))
-        a1h, a1l = split(jnp.where(is_first, other, mine))
-        b0 = matmul(high[0:256, 0:256], a0h) + (
-            matmul(high[0:256, 0:256], a0l) + matmul(low[0:256, 0:256], a0h)
+        at = slice(256 * m, 256 * m + 256)
+        mine, other = column(m)
+        a0 = jnp.where(is_first, mine, other)
+        a1 = jnp.where(is_first, other, mine)
+        b0 = product([p[0:256, 0:256] for p in w], split(a0))
+        b1 = product([p[256:512] for p in w], split(jnp.concatenate([a0, a1], axis=0)))
+        b0, b1 = split(b0), split(b1)
+        z0 = product([p[0:256] for p in turned], [jnp.concatenate(p, axis=0) for p in zip(b0, b1)])
+        z1 = product([p[256:512, 256:512] for p in turned], b1)
+        zh, zl = split(jnp.concatenate([z0, z1], axis=0))
+        z_ref[0:512, at] = zh
+        z_ref[512:1024, at] = zl
+        z_ref[1024:1536, at] = zh
+
+
+def update_kernel(
+    place, x_ref, g_ref, w0_ref, w1_ref, under_ref, lt0_ref, lt1_ref, mine_ref, other_ref, out_ref,
+    old, new, tiles, wt, z, near, old_sem, new_sem, tile_sem, near_sem,
+):
+    row, col = place[0], place[1]
+
+    def load(l, mh):
+        at = pl.ds(l * 256, 256)
+        return pltpu.make_async_copy(
+            x_ref.at[at, mh], old.at[l, :, pl.ds(128 * mh, 128)], old_sem.at[l, mh]
         )
-        ah = jnp.concatenate([a0h, a1h], axis=0)
-        al = jnp.concatenate([a0l, a1l], axis=0)
-        b1 = matmul(high[256:512], ah) + (matmul(high[256:512], al) + matmul(low[256:512], ah))
-        bh, bl = split(jnp.concatenate([b0, b1], axis=0))
-        bc[0:512, 256 * m : 256 * m + 256] = bh
-        bc[512:1024, 256 * m : 256 * m + 256] = bl
-        bc[1024:1536, 256 * m : 256 * m + 256] = bh
+
+    def fetch(l, k):
+        return pltpu.make_async_copy(
+            g_ref.at[position(row, l, k)], tiles.at[l, k], tile_sem.at[l, k]
+        )
+
+    def store(l, mh):
+        at = pl.ds(l * 256, 256)
+        return pltpu.make_async_copy(
+            new.at[l % 2, :, pl.ds(128 * mh, 128)], out_ref.at[at, mh], new_sem.at[l % 2, mh]
+        )
+
+    def take(i, m):
+        source = (mine_ref, other_ref)[i]
+        return pltpu.make_async_copy(source.at[m], near.at[i, m], near_sem.at[i, m])
+
+    for m in range(4):
+        for i in range(2):
+            take(i, m).start()
+
+    @pl.loop(0, 8)
+    def _(l):
+        for k in range(2):
+            fetch(l, k).start()
+        for mh in range(8):
+            load(l, mh).start()
+
+    def column(m):
+        for i in range(2):
+            take(i, m).wait()
+        return near[0, m], near[1, m]
+
+    columns(lax.rem(row, 2) == 0, w0_ref, w1_ref, under_ref, column, wt, z)
 
     @pl.loop(0, 8)
     def _(l):
         for k in range(2):
             fetch(l, k).wait()
-        x0h, x0l = split(tiles[l, 0])
-        x1h, x1l = split(tiles[l, 1])
-        wh, wl = wt[0:512, :], wt[512:1024, :]
-        b0 = matmul(x0h, wh[0:256, 0:256]) + (
-            matmul(x0l, wh[0:256, 0:256]) + matmul(x0h, wl[0:256, 0:256])
-        )
-        xh = jnp.concatenate([x0h, x1h], axis=1)
-        xl = jnp.concatenate([x0l, x1l], axis=1)
-        b1 = matmul(xh, wh[:, 256:512]) + (
-            matmul(xl, wh[:, 256:512]) + matmul(xh, wl[:, 256:512])
-        )
-        bh, bl = split(jnp.concatenate([b0, b1], axis=1))
-        left = jnp.concatenate([bh, bh, bl], axis=1)
+        xh, xl = split(jnp.concatenate([tiles[l, 0], tiles[l, 1]], axis=1))
+        left = jnp.concatenate([xh, xh, xl], axis=1)
 
         for mh in range(8):
             load(l, mh).wait()
@@ -243,23 +252,31 @@
                 store(l - 2, mh).wait()
 
         slot = l % 2
-        for m in range(4):
+        for m in range(1, 4):
             at = slice(256 * m, 256 * m + 256)
-            new[slot, :, at] = old[l, :, at] - matmul(left, bc[:, at])
-
-        @pl.when(col <= 1)
-        def _():
-            new[slot, :, 0:256] = jnp.where(col == 0, b0, b1)
+            new[slot, :, at] = old[l, :, at] - matmul(left, z[:, at])
+
+        @pl.when(col > 1)
+        def _():
+            new[slot, :, 0:256] = old[l, :, 0:256] - matmul(left, z[:, 0:256])
+
+        @pl.when(col == 0)
+        def _():
+            x = (xh[:, 0:256], xl[:, 0:256])
+            new[slot, :, 0:256] = product(x, (wt[0:256, 0:256], wt[512:768, 0:256]))
+
+        @pl.when(col == 1)
+        def _():
+            new[slot, :, 0:256] = product((xh, xl), (wt[0:512, 256:512], wt[512:1024, 256:512]))
 
         @pl.when((l == 0) & (row <= 1))
         def _():
-            zero = jnp.zeros((256, 256), F32)
             new[slot, :, 256:1024] = jnp.zeros((256, 768), F32)
-            new[slot, :, 0:256] = jnp.where(
-                row == 0,
-                jnp.where(col == 0, lt0_ref[...].T, zero),
-                jnp.where(col == 0, b0, jnp.where(col == 1, lt1_ref[...].T, zero)),
-            )
+
+            @pl.when((row == 0) | (col > 0))
+            def _():
+                own = jnp.where(row == 0, lt0_ref[...].T, lt1_ref[...].T)
+                new[slot, :, 0:256] = jnp.where(col == row, own, 0.0)
 
         for mh in range(8):
             store(l, mh).start()
@@ -281,7 +298,7 @@
     hbm = pl.BlockSpec(memory_space=pl.ANY)
     return pl.pallas_call(
         update_kernel,
-        in_specs=[pl.BlockSpec(memory_space=pltpu.SMEM), hbm, hbm] + [vmem] * 7,
+        in_specs=[pl.BlockSpec(memory_space=pltpu.SMEM), hbm, hbm] + [vmem] * 5 + [hbm] * 2,
         out_specs=hbm,
         out_shape=jax.ShapeDtypeStruct((2048, 8, 128), F32),
         scratch_shapes=[
@@ -290,9 +307,11 @@
             pltpu.VMEM((8, 2, 256, 256), F32),
             pltpu.VMEM((1024, 512), BF16),
             pltpu.VMEM((1536, 1024), BF16),
+            pltpu.VMEM((2, 4, 256, 256), F32),
             pltpu.SemaphoreType.DMA((8, 8)),
             pltpu.SemaphoreType.DMA((2, 8)),
             pltpu.SemaphoreType.DMA((8, 2)),
+            pltpu.SemaphoreType.DMA((2, 4)),
         ],
         compiler_params=pltpu.CompilerParams(vmem_limit_bytes=48 * MIB),
     )(place, x, gathered, w0, w1, under, lt0, lt1, mine, other)

time: 129 us -> 129 us (level)
  no operation moved by 1% of the time
where the time goes in v3:
time: 129 us
  Pallas kernels  40 us (31%)
  starting transfers between devices  27.9 us (22%)
  blocking collectives  25.8 us (20%)
  waiting for transfers between devices  17.6 us (14%)
  between operations  13.5 us (10%)
  other arithmetic  2.98 us (2%)
    pallas_call x1, Pallas kernels, factor(): pl.pallas_call(factor_kernel, out_shape=[square] * 5, scratch_shapes=[plt...  19.8 us
    pallas_call x1, Pallas kernels, update(): pl.pallas_call(update_kernel, in_specs=[pl.BlockSpec(memory_space=pltpu.S...  17.4 us
    all_to_all x1, blocking collectives, shards(): d = lax.all_to_all(tile.reshape(16, 16, 256), 'col', 0, 0, tiled=True)[0:2]  17.2 us
    ppermute x4, starting transfers between devices, shards(): lax.ppermute(turned[m], ('row', 'col'), scatter_pairs(m))  15 us
    all_to_all x1, waiting for transfers between devices, shards(): lax.all_to_all(jnp.broadcast_to(d[None], (16, 3, 16, 256)), 'col', 0, 0,...  12.8 us
    all_to_all x1, blocking collectives, shards(): lax.all_to_all(jnp.broadcast_to(d[None], (8, 2, 16, 256)), 'row', 0, 0, t...  8.57 us
    ppermute x3, starting transfers between devices, along_z(): return lax.ppermute(array, 'row', [(k, 2 * step + k) for k in range(2)])  7.34 us
    all_to_all x1, starting transfers between devices, shards(): lax.all_to_all(jnp.broadcast_to(d[None], (16, 3, 16, 256)), 'col', 0, 0,...  4.01 us
  transfers between devices with their start and end apart: 10, of which 3 were waited for; matrix products, arithmetic and copies ran while one was open for 3% of the time, Pallas kernels for 15%

profile of v3, /device:TPU:1, one launch (start us, length us, event | category | flops | bytes accessed | tf_op | source)
XLA Modules:
  0.0 128.9 jit_solution(10094663121355535112)
XLA Ops:
  6.5 0.0 all-gather.3.cloned.1.call-start
  6.5 2.8 %shard_map.17 = (f32[256,256]{1,0:T(8,128)}, f32[4,256,256]{2,1,0:T(8,128)}, f32[256,256]{1,0:T(8,128)}, f32[256,256]{1,0:T(8,128)}, f32[256,256]{1,0:T(8,128)}, /*index=5*/f32[256,256]{1,0:T(8,128)}) custom-call(f32[16384,128]{1,0:T(8,128)} %bitcast.13), custom_call_target="tpu_custom_call" | custom-call | tf_op jit(solution)/shard_map/pallas_call | solution.py:50
  9.3 4.6 %collective-permute-start = (f32[256,256]{1,0:T(8,128)}, f32[256,256]{1,0:T(8,128)S(1)}, u32[]{:S(2)}, u32[]{:S(2)}) collective-permute-start(f32[256,256]{1,0:T(8,128)} %get-tuple-element.29), channel_id=1, source_target_pairs={{0,0},{1,17},{2,34},{3,51},{4,68},{5,85},{6,102},{7,119},{8,8},{9,... | collective-permute-start | bytes 786440 | tf_op jit(solution)/shard_map/ppermute | solution.py:340
  14.0 4.7 %collective-permute-start.1 = (f32[256,256]{1,0:T(8,128)}, f32[256,256]{1,0:T(8,128)S(1)}, u32[]{:S(2)}, u32[]{:S(2)}) collective-permute-start(f32[256,256]{1,0:T(8,128)} %get-tuple-element.30), channel_id=1, source_target_pairs={{0,2},{1,19},{2,32},{3,49},{4,70},{5,87},{6,100},{7,117},{8,10},{9... | collective-permute-start | bytes 786440 | tf_op jit(solution)/shard_map/ppermute | solution.py:340
  18.7 3.9 %collective-permute-start.2 = (f32[256,256]{1,0:T(8,128)}, f32[256,256]{1,0:T(8,128)S(1)}, u32[]{:S(2)}, u32[]{:S(2)}) collective-permute-start(f32[256,256]{1,0:T(8,128)} %get-tuple-element.31), channel_id=1, source_target_pairs={{0,4},{1,21},{2,38},{3,55},{4,72},{5,89},{6,106},{7,123},{8,12},{9... | collective-permute-start | bytes 786440 | tf_op jit(solution)/shard_map/ppermute | solution.py:340
  22.5 1.8 %collective-permute-start.3 = (f32[256,256]{1,0:T(8,128)}, f32[256,256]{1,0:T(8,128)S(1)}, u32[]{:S(2)}, u32[]{:S(2)}) collective-permute-start(f32[256,256]{1,0:T(8,128)} %get-tuple-element.32), channel_id=1, source_target_pairs={{0,6},{1,23},{2,36},{3,53},{4,74},{5,91},{6,104},{7,121},{8,14},{9... | collective-permute-start | bytes 786440 | tf_op jit(solution)/shard_map/ppermute | solution.py:340
  24.4 17.2 %all_to_all.15 = f32[16,16,256]{2,1,0:T(8,128)S(1)} all-to-all(f32[16,16,256]{2,1,0:T(8,128)} %bitcast.16), channel_id=1, replica_groups=mesh['row'=8,'col'=16] {'col'}, dimensions={0} | all-to-all | bytes 524288 | tf_op jit(solution)/shard_map/all_to_all | solution.py:341
  41.6 0.0 collective-permute-done
  41.6 0.0 collective-permute-done.1
  41.7 0.0 collective-permute-done.2
  41.7 0.0 collective-permute-done.3
  41.7 0.8 add_add_fusion
  42.4 0.0 all-gather.3.cloned.1.call-update
  42.5 8.6 %all_to_all.16 = f32[8,2,16,256]{3,2,1,0:T(8,128)S(1)} all-to-all(f32[8,2,16,256]{3,2,1,0:T(8,128)S(1)} %broadcast_in_dim.4), channel_id=1, replica_groups=mesh['row'=8,'col'=16] {'row'}, dimensions={0} | all-to-all | bytes 524288 | tf_op jit(solution)/shard_map/all_to_all | solution.py:347
  51.1 2.8 %collective-permute-start.6 = (f32[4,256,256]{2,1,0:T(8,128)}, f32[4,256,256]{2,1,0:T(8,128)S(1)}, u32[]{:S(2)}, u32[]{:S(2)}) collective-permute-start(f32[4,256,256]{2,1,0:T(8,128)} %get-tuple-element.44), channel_id=1, source_target_pairs={{0,64},{16,80},{1,65},{17,81},{2,66},{18,82},{3,67},{19,83},{4,68}... | collective-permute-start | bytes 3145736 | tf_op jit(solution)/shard_map/ppermute | solution.py:331
  53.9 2.3 %collective-permute-start.5 = (f32[4,256,256]{2,1,0:T(8,128)}, f32[4,256,256]{2,1,0:T(8,128)}, u32[]{:S(2)}, u32[]{:S(2)}) collective-permute-start(f32[4,256,256]{2,1,0:T(8,128)} %get-tuple-element.44), channel_id=1, source_target_pairs={{0,96},{16,112},{1,97},{17,113},{2,98},{18,114},{3,99},{19,115},{4... | collective-permute-start | bytes 3145736 | tf_op jit(solution)/shard_map/ppermute | solution.py:331
  56.2 2.3 %collective-permute-start.4 = (f32[4,256,256]{2,1,0:T(8,128)}, f32[4,256,256]{2,1,0:T(8,128)}, u32[]{:S(2)}, u32[]{:S(2)}) collective-permute-start(f32[4,256,256]{2,1,0:T(8,128)} %get-tuple-element.44), channel_id=1, source_target_pairs={{0,32},{16,48},{1,33},{17,49},{2,34},{18,50},{3,35},{19,51},{4,36}... | collective-permute-start | bytes 3145736 | tf_op jit(solution)/shard_map/ppermute | solution.py:331
  58.4 1.0 broadcast_in_dim.5
  59.4 4.0 %all-to-all-start.2 = ((f32[16,3,16,256]{3,2,1,0:T(8,128)}), f32[16,3,16,256]{3,2,1,0:T(8,128)S(1)}, u32[]{:S(2)}, u32[]{:S(2)}) async-start(f32[16,3,16,256]{3,2,1,0:T(8,128)} %broadcast_in_dim.5), calls=%async_computation.2 | async-start | bytes 1572864 | tf_op jit(solution)/shard_map/all_to_all | solution.py:351
  63.5 12.8 %all-to-all-done.2.d_ref = f32[16,3,16,256]{3,2,1,0:T(8,128)S(1)} async-done(((f32[16,3,16,256]{3,2,1,0:T(8,128)}), f32[16,3,16,256]{3,2,1,0:T(8,128)S(1)}, u32[]{:S(2)}, u32[]{:S(2)}) %all-to-all-start.2) | async-done | bytes 786464 | tf_op jit(solution)/shard_map/all_to_all | solution.py:351
  76.2 19.8 %shard_map.18 = (f32[256,256]{1,0:T(8,128)S(1)}, f32[256,256]{1,0:T(8,128)S(1)}, f32[256,256]{1,0:T(8,128)S(1)}, f32[256,256]{1,0:T(8,128)S(1)}, f32[256,256]{1,0:T(8,128)S(1)}) custom-call(f32[16,3,16,256]{3,2,1,0:T(8,128)S(1)} %all-to-all-done.2.d_ref), custom_call_target="tpu_custom_call" | custom-call | tf_op jit(solution)/shard_map/pallas_call | solution.py:153
  96.1 0.0 collective-permute-done.6
  96.1 0.0 collective-permute-done.5
  96.1 2.6 %collective-permute-done.4 = f32[4,256,256]{2,1,0:T(8,128)} collective-permute-done((f32[4,256,256]{2,1,0:T(8,128)}, f32[4,256,256]{2,1,0:T(8,128)}, u32[]{:S(2)}, u32[]{:S(2)}) %collective-permute-start.4) | collective-permute-done | bytes 1048608 | tf_op jit(solution)/shard_map/ppermute | solution.py:331
  98.7 2.1 %add_select_fusion.mine_ref = f32[4,256,256]{2,1,0:T(8,128)S(1)} fusion(f32[4,256,256]{2,1,0:T(8,128)} %get-tuple-element.44, f32[4,256,256]{2,1,0:T(8,128)S(1)} %collective-permute-done.6, f32[4,256,256]{2,1,0:T(8,128)} %collective-permute-done.4, f32[4,256,256]{2,1,0:T(8,128)} %collective-permute-done.5, pred[]{:T(512)S(6)} %lt.3), kind=kLoop, calls=%fused_computation | loop fusion | flops 786432 | bytes 5242881 | tf_op jit(solution)/shard_map/jit(_where)/select_n | solution.py:355
  100.8 1.5 %collective-permute-start.7 = (f32[4,256,256]{2,1,0:T(8,128)S(1)}, f32[4,256,256]{2,1,0:T(8,128)S(1)}, u32[]{:S(2)}, u32[]{:S(2)}) collective-permute-start(f32[4,256,256]{2,1,0:T(8,128)S(1)} %add_select_fusion.mine_ref), channel_id=1, source_target_pairs={{0,16},{16,0},{32,48},{48,32},{64,80},{80,64},{96,112},{112,96},{1... | collective-permute-start | bytes 3145736 | tf_op jit(solution)/shard_map/ppermute | solution.py:356
  102.3 0.1 pad_add_fusion.place
  102.4 2.2 %collective-permute-done.7.other_ref = f32[4,256,256]{2,1,0:T(8,128)S(1)} collective-permute-done((f32[4,256,256]{2,1,0:T(8,128)S(1)}, f32[4,256,256]{2,1,0:T(8,128)S(1)}, u32[]{:S(2)}, u32[]{:S(2)}) %collective-permute-start.7) | collective-permute-done | bytes 1048608 | tf_op jit(solution)/shard_map/ppermute | solution.py:356
  104.6 0.0 all-gather.3.cloned.1.call-done
  104.6 17.4 %shard_map.19 = f32[2048,8,128]{2,1,0:T(8,128)} custom-call(s32[2]{0:T(128)S(1)} %pad_add_fusion.place, f32[2048,8,128]{2,1,0:T(8,128)} %bitcast.14, f32[16,256,256]{2,1,0:T(8,128)} %bitcast.15, f32[256,256]{1,0:T(8,128)S(1)} %get-tuple-element.43.w0_ref, f32[256,256]{1,0:T(8,128)S(1)} %get-tuple-element.46.w1_ref, ...), custom_call_target="tpu_custom_call" | custom-call | tf_op jit(solution)/shard_map/pallas_call | solution.py:299
  (4 shorter events, 0.0 us)
Async XLA Ops:
  6.5 98.1 %all-gather.3.cloned.1.call-start = ((), (), s32[]{:S(2)}) async-start(), calls=%async_computation.3 | async-start | bytes 4456448 | tf_op jit(solution)/shard_map/all_gather | solution.py:345
  9.3 32.3 %collective-permute-start = (f32[256,256]{1,0:T(8,128)}, f32[256,256]{1,0:T(8,128)S(1)}, u32[]{:S(2)}, u32[]{:S(2)}) collective-permute-start(f32[256,256]{1,0:T(8,128)} %get-tuple-element.29), channel_id=1, source_target_pairs={{0,0},{1,17},{2,34},{3,51},{4,68},{5,85},{6,102},{7,119},{8,8},{9,... | collective-permute-start | bytes 786440 | tf_op jit(solution)/shard_map/ppermute | solution.py:340
  14.0 27.7 %collective-permute-start.1 = (f32[256,256]{1,0:T(8,128)}, f32[256,256]{1,0:T(8,128)S(1)}, u32[]{:S(2)}, u32[]{:S(2)}) collective-permute-start(f32[256,256]{1,0:T(8,128)} %get-tuple-element.30), channel_id=1, source_target_pairs={{0,2},{1,19},{2,32},{3,49},{4,70},{5,87},{6,100},{7,117},{8,10},{9... | collective-permute-start | bytes 786440 | tf_op jit(solution)/shard_map/ppermute | solution.py:340
  18.7 23.0 %collective-permute-start.2 = (f32[256,256]{1,0:T(8,128)}, f32[256,256]{1,0:T(8,128)S(1)}, u32[]{:S(2)}, u32[]{:S(2)}) collective-permute-start(f32[256,256]{1,0:T(8,128)} %get-tuple-element.31), channel_id=1, source_target_pairs={{0,4},{1,21},{2,38},{3,55},{4,72},{5,89},{6,106},{7,123},{8,12},{9... | collective-permute-start | bytes 786440 | tf_op jit(solution)/shard_map/ppermute | solution.py:340
  22.5 19.1 %collective-permute-start.3 = (f32[256,256]{1,0:T(8,128)}, f32[256,256]{1,0:T(8,128)S(1)}, u32[]{:S(2)}, u32[]{:S(2)}) collective-permute-start(f32[256,256]{1,0:T(8,128)} %get-tuple-element.32), channel_id=1, source_target_pairs={{0,6},{1,23},{2,36},{3,53},{4,74},{5,91},{6,104},{7,121},{8,14},{9... | collective-permute-start | bytes 786440 | tf_op jit(solution)/shard_map/ppermute | solution.py:340
  51.1 45.0 %collective-permute-start.6 = (f32[4,256,256]{2,1,0:T(8,128)}, f32[4,256,256]{2,1,0:T(8,128)S(1)}, u32[]{:S(2)}, u32[]{:S(2)}) collective-permute-start(f32[4,256,256]{2,1,0:T(8,128)} %get-tuple-element.44), channel_id=1, source_target_pairs={{0,64},{16,80},{1,65},{17,81},{2,66},{18,82},{3,67},{19,83},{4,68}... | collective-permute-start | bytes 3145736 | tf_op jit(solution)/shard_map/ppermute | solution.py:331
  53.9 42.2 %collective-permute-start.5 = (f32[4,256,256]{2,1,0:T(8,128)}, f32[4,256,256]{2,1,0:T(8,128)}, u32[]{:S(2)}, u32[]{:S(2)}) collective-permute-start(f32[4,256,256]{2,1,0:T(8,128)} %get-tuple-element.44), channel_id=1, source_target_pairs={{0,96},{16,112},{1,97},{17,113},{2,98},{18,114},{3,99},{19,115},{4... | collective-permute-start | bytes 3145736 | tf_op jit(solution)/shard_map/ppermute | solution.py:331
  56.2 42.5 %collective-permute-start.4 = (f32[4,256,256]{2,1,0:T(8,128)}, f32[4,256,256]{2,1,0:T(8,128)}, u32[]{:S(2)}, u32[]{:S(2)}) collective-permute-start(f32[4,256,256]{2,1,0:T(8,128)} %get-tuple-element.44), channel_id=1, source_target_pairs={{0,32},{16,48},{1,33},{17,49},{2,34},{18,50},{3,35},{19,51},{4,36}... | collective-permute-start | bytes 3145736 | tf_op jit(solution)/shard_map/ppermute | solution.py:331
  59.4 16.8 %all-to-all-start.2 = ((f32[16,3,16,256]{3,2,1,0:T(8,128)}), f32[16,3,16,256]{3,2,1,0:T(8,128)S(1)}, u32[]{:S(2)}, u32[]{:S(2)}) async-start(f32[16,3,16,256]{3,2,1,0:T(8,128)} %broadcast_in_dim.5), calls=%async_computation.2 | async-start | bytes 1572864 | tf_op jit(solution)/shard_map/all_to_all | solution.py:351
  100.8 3.8 %collective-permute-start.7 = (f32[4,256,256]{2,1,0:T(8,128)S(1)}, f32[4,256,256]{2,1,0:T(8,128)S(1)}, u32[]{:S(2)}, u32[]{:S(2)}) collective-permute-start(f32[4,256,256]{2,1,0:T(8,128)S(1)} %add_select_fusion.mine_ref), channel_id=1, source_target_pairs={{0,16},{16,0},{32,48},{48,32},{64,80},{80,64},{96,112},{112,96},{1... | collective-permute-start | bytes 3145736 | tf_op jit(solution)/shard_map/ppermute | solution.py:356
Sparse Core Ops, SparseCore 0:
  42.6 52.1 all-gather.2

commit v4 on v3

--- a/solution.py
+++ b/solution.py
@@ -163,7 +163,7 @@
     return matmul(a[0], b[0]) + (matmul(a[0], b[1]) + matmul(a[1], b[0]))
 
 
-def columns(is_first, w0_ref, w1_ref, under_ref, column, wt_ref, z_ref):
+def columns(is_first, w0_ref, w1_ref, under_ref, mine_ref, other_ref, wt_ref, z_ref):
     w = jnp.concatenate(
         [
             jnp.concatenate([w0_ref[...], jnp.zeros((256, 256), F32)], axis=1),
@@ -177,7 +177,7 @@
     w = split(w)
     for m in range(4):
         at = slice(256 * m, 256 * m + 256)
-        mine, other = column(m)
+        mine, other = mine_ref[m], other_ref[m]
         a0 = jnp.where(is_first, mine, other)
         a1 = jnp.where(is_first, other, mine)
         b0 = product([p[0:256, 0:256] for p in w], split(a0))
@@ -193,7 +193,7 @@
 
 def update_kernel(
     place, x_ref, g_ref, w0_ref, w1_ref, under_ref, lt0_ref, lt1_ref, mine_ref, other_ref, out_ref,
-    old, new, tiles, wt, z, near, old_sem, new_sem, tile_sem, near_sem,
+    old, new, tiles, wt, z, old_sem, new_sem, tile_sem,
 ):
     row, col = place[0], place[1]
 
@@ -213,14 +213,6 @@
         return pltpu.make_async_copy(
             new.at[l % 2, :, pl.ds(128 * mh, 128)], out_ref.at[at, mh], new_sem.at[l % 2, mh]
         )
-
-    def take(i, m):
-        source = (mine_ref, other_ref)[i]
-        return pltpu.make_async_copy(source.at[m], near.at[i, m], near_sem.at[i, m])
-
-    for m in range(4):
-        for i in range(2):
-            take(i, m).start()
 
     @pl.loop(0, 8)
     def _(l):
@@ -229,12 +221,8 @@
         for mh in range(8):
             load(l, mh).start()
 
-    def column(m):
-        for i in range(2):
-            take(i, m).wait()
-        return near[0, m], near[1, m]
-
-    columns(lax.rem(row, 2) == 0, w0_ref, w1_ref, under_ref, column, wt, z)
+    is_first = lax.rem(row, 2) == 0
+    columns(is_first, w0_ref, w1_ref, under_ref, mine_ref, other_ref, wt, z)
 
     @pl.loop(0, 8)
     def _(l):
@@ -298,7 +286,7 @@
     hbm = pl.BlockSpec(memory_space=pl.ANY)
     return pl.pallas_call(
         update_kernel,
-        in_specs=[pl.BlockSpec(memory_space=pltpu.SMEM), hbm, hbm] + [vmem] * 5 + [hbm] * 2,
+        in_specs=[pl.BlockSpec(memory_space=pltpu.SMEM), hbm, hbm] + [vmem] * 7,
         out_specs=hbm,
         out_shape=jax.ShapeDtypeStruct((2048, 8, 128), F32),
         scratch_shapes=[
@@ -307,11 +295,9 @@
             pltpu.VMEM((8, 2, 256, 256), F32),
             pltpu.VMEM((1024, 512), BF16),
             pltpu.VMEM((1536, 1024), BF16),
-            pltpu.VMEM((2, 4, 256, 256), F32),
             pltpu.SemaphoreType.DMA((8, 8)),
             pltpu.SemaphoreType.DMA((2, 8)),
             pltpu.SemaphoreType.DMA((8, 2)),
-            pltpu.SemaphoreType.DMA((2, 4)),
         ],
         compiler_params=pltpu.CompilerParams(vmem_limit_bytes=48 * MIB),
     )(place, x, gathered, w0, w1, under, lt0, lt1, mine, other)

time: 129 us -> 128 us (level)
  Pallas kernels: 40 us -> 38.7 us
    pallas_call x1, Pallas kernels: 17.4 us -> 16 us  [update(): pl.pallas_call(update_kernel, in_specs=[pl.BlockSpec(memory_space=pltpu.S...]
  transfers between devices with their start and end apart: 10 -> 10, of which waited for: 3 -> 3; matrix products, arithmetic and copies ran while one was open for 3% -> 3% of each run, Pallas kernels for 15% -> 16%
where the time goes in v4:
time: 128 us
  Pallas kernels  38.7 us (30%)
  starting transfers between devices  27.9 us (22%)
  blocking collectives  25.8 us (20%)
  waiting for transfers between devices  17.6 us (14%)
  between operations  13.5 us (11%)
  other arithmetic  2.98 us (2%)
    pallas_call x1, Pallas kernels, factor(): pl.pallas_call(factor_kernel, out_shape=[square] * 5, scratch_shapes=[plt...  19.8 us
    all_to_all x1, blocking collectives, shards(): d = lax.all_to_all(tile.reshape(16, 16, 256), 'col', 0, 0, tiled=True)[0:2]  17.2 us
    pallas_call x1, Pallas kernels, update(): pl.pallas_call(update_kernel, in_specs=[pl.BlockSpec(memory_space=pltpu.S...  16 us
    ppermute x4, starting transfers between devices, shards(): lax.ppermute(turned[m], ('row', 'col'), scatter_pairs(m))  15 us
    all_to_all x1, waiting for transfers between devices, shards(): lax.all_to_all(jnp.broadcast_to(d[None], (16, 3, 16, 256)), 'col', 0, 0,...  12.8 us
    all_to_all x1, blocking collectives, shards(): lax.all_to_all(jnp.broadcast_to(d[None], (8, 2, 16, 256)), 'row', 0, 0, t...  8.57 us
    ppermute x3, starting transfers between devices, along_z(): return lax.ppermute(array, 'row', [(k, 2 * step + k) for k in range(2)])  7.34 us
    all_to_all x1, starting transfers between devices, shards(): lax.all_to_all(jnp.broadcast_to(d[None], (16, 3, 16, 256)), 'col', 0, 0,...  4.01 us
  transfers between devices with their start and end apart: 10, of which 3 were waited for; matrix products, arithmetic and copies ran while one was open for 3% of the time, Pallas kernels for 16%

profile of v4, /device:TPU:1, one launch (start us, length us, event | category | flops | bytes accessed | tf_op | source)
XLA Modules:
  0.0 127.5 jit_solution(807470828208352921)
XLA Ops:
  6.5 0.0 all-gather.3.cloned.1.call-start
  6.5 2.8 %shard_map.17 = (f32[256,256]{1,0:T(8,128)}, f32[4,256,256]{2,1,0:T(8,128)}, f32[256,256]{1,0:T(8,128)}, f32[256,256]{1,0:T(8,128)}, f32[256,256]{1,0:T(8,128)}, /*index=5*/f32[256,256]{1,0:T(8,128)}) custom-call(f32[16384,128]{1,0:T(8,128)} %bitcast.13), custom_call_target="tpu_custom_call" | custom-call | tf_op jit(solution)/shard_map/pallas_call | solution.py:50
  9.3 4.6 %collective-permute-start = (f32[256,256]{1,0:T(8,128)}, f32[256,256]{1,0:T(8,128)S(1)}, u32[]{:S(2)}, u32[]{:S(2)}) collective-permute-start(f32[256,256]{1,0:T(8,128)} %get-tuple-element.29), channel_id=1, source_target_pairs={{0,0},{1,17},{2,34},{3,51},{4,68},{5,85},{6,102},{7,119},{8,8},{9,... | collective-permute-start | bytes 786440 | tf_op jit(solution)/shard_map/ppermute | solution.py:326
  14.0 4.7 %collective-permute-start.1 = (f32[256,256]{1,0:T(8,128)}, f32[256,256]{1,0:T(8,128)S(1)}, u32[]{:S(2)}, u32[]{:S(2)}) collective-permute-start(f32[256,256]{1,0:T(8,128)} %get-tuple-element.30), channel_id=1, source_target_pairs={{0,2},{1,19},{2,32},{3,49},{4,70},{5,87},{6,100},{7,117},{8,10},{9... | collective-permute-start | bytes 786440 | tf_op jit(solution)/shard_map/ppermute | solution.py:326
  18.7 3.9 %collective-permute-start.2 = (f32[256,256]{1,0:T(8,128)}, f32[256,256]{1,0:T(8,128)S(1)}, u32[]{:S(2)}, u32[]{:S(2)}) collective-permute-start(f32[256,256]{1,0:T(8,128)} %get-tuple-element.31), channel_id=1, source_target_pairs={{0,4},{1,21},{2,38},{3,55},{4,72},{5,89},{6,106},{7,123},{8,12},{9... | collective-permute-start | bytes 786440 | tf_op jit(solution)/shard_map/ppermute | solution.py:326
  22.5 1.8 %collective-permute-start.3 = (f32[256,256]{1,0:T(8,128)}, f32[256,256]{1,0:T(8,128)S(1)}, u32[]{:S(2)}, u32[]{:S(2)}) collective-permute-start(f32[256,256]{1,0:T(8,128)} %get-tuple-element.32), channel_id=1, source_target_pairs={{0,6},{1,23},{2,36},{3,53},{4,74},{5,91},{6,104},{7,121},{8,14},{9... | collective-permute-start | bytes 786440 | tf_op jit(solution)/shard_map/ppermute | solution.py:326
  24.4 17.2 %all_to_all.15 = f32[16,16,256]{2,1,0:T(8,128)S(1)} all-to-all(f32[16,16,256]{2,1,0:T(8,128)} %bitcast.16), channel_id=1, replica_groups=mesh['row'=8,'col'=16] {'col'}, dimensions={0} | all-to-all | bytes 524288 | tf_op jit(solution)/shard_map/all_to_all | solution.py:327
  41.6 0.0 collective-permute-done
  41.6 0.0 collective-permute-done.1
  41.7 0.0 collective-permute-done.2
  41.7 0.0 collective-permute-done.3
  41.7 0.8 add_add_fusion
  42.4 0.0 all-gather.3.cloned.1.call-update
  42.5 8.6 %all_to_all.16 = f32[8,2,16,256]{3,2,1,0:T(8,128)S(1)} all-to-all(f32[8,2,16,256]{3,2,1,0:T(8,128)S(1)} %broadcast_in_dim.4), channel_id=1, replica_groups=mesh['row'=8,'col'=16] {'row'}, dimensions={0} | all-to-all | bytes 524288 | tf_op jit(solution)/shard_map/all_to_all | solution.py:333
  51.1 2.8 %collective-permute-start.6 = (f32[4,256,256]{2,1,0:T(8,128)}, f32[4,256,256]{2,1,0:T(8,128)S(1)}, u32[]{:S(2)}, u32[]{:S(2)}) collective-permute-start(f32[4,256,256]{2,1,0:T(8,128)} %get-tuple-element.44), channel_id=1, source_target_pairs={{0,64},{16,80},{1,65},{17,81},{2,66},{18,82},{3,67},{19,83},{4,68}... | collective-permute-start | bytes 3145736 | tf_op jit(solution)/shard_map/ppermute | solution.py:317
  53.9 2.3 %collective-permute-start.5 = (f32[4,256,256]{2,1,0:T(8,128)}, f32[4,256,256]{2,1,0:T(8,128)}, u32[]{:S(2)}, u32[]{:S(2)}) collective-permute-start(f32[4,256,256]{2,1,0:T(8,128)} %get-tuple-element.44), channel_id=1, source_target_pairs={{0,96},{16,112},{1,97},{17,113},{2,98},{18,114},{3,99},{19,115},{4... | collective-permute-start | bytes 3145736 | tf_op jit(solution)/shard_map/ppermute | solution.py:317
  56.2 2.3 %collective-permute-start.4 = (f32[4,256,256]{2,1,0:T(8,128)}, f32[4,256,256]{2,1,0:T(8,128)}, u32[]{:S(2)}, u32[]{:S(2)}) collective-permute-start(f32[4,256,256]{2,1,0:T(8,128)} %get-tuple-element.44), channel_id=1, source_target_pairs={{0,32},{16,48},{1,33},{17,49},{2,34},{18,50},{3,35},{19,51},{4,36}... | collective-permute-start | bytes 3145736 | tf_op jit(solution)/shard_map/ppermute | solution.py:317
  58.4 1.0 broadcast_in_dim.5
  59.4 4.0 %all-to-all-start.2 = ((f32[16,3,16,256]{3,2,1,0:T(8,128)}), f32[16,3,16,256]{3,2,1,0:T(8,128)S(1)}, u32[]{:S(2)}, u32[]{:S(2)}) async-start(f32[16,3,16,256]{3,2,1,0:T(8,128)} %broadcast_in_dim.5), calls=%async_computation.2 | async-start | bytes 1572864 | tf_op jit(solution)/shard_map/all_to_all | solution.py:337
  63.5 12.8 %all-to-all-done.2.d_ref = f32[16,3,16,256]{3,2,1,0:T(8,128)S(1)} async-done(((f32[16,3,16,256]{3,2,1,0:T(8,128)}), f32[16,3,16,256]{3,2,1,0:T(8,128)S(1)}, u32[]{:S(2)}, u32[]{:S(2)}) %all-to-all-start.2) | async-done | bytes 786464 | tf_op jit(solution)/shard_map/all_to_all | solution.py:337
  76.2 19.8 %shard_map.18 = (f32[256,256]{1,0:T(8,128)S(1)}, f32[256,256]{1,0:T(8,128)S(1)}, f32[256,256]{1,0:T(8,128)S(1)}, f32[256,256]{1,0:T(8,128)S(1)}, f32[256,256]{1,0:T(8,128)S(1)}) custom-call(f32[16,3,16,256]{3,2,1,0:T(8,128)S(1)} %all-to-all-done.2.d_ref), custom_call_target="tpu_custom_call" | custom-call | tf_op jit(solution)/shard_map/pallas_call | solution.py:153
  96.1 0.0 collective-permute-done.6
  96.1 0.0 collective-permute-done.5
  96.1 2.6 %collective-permute-done.4 = f32[4,256,256]{2,1,0:T(8,128)} collective-permute-done((f32[4,256,256]{2,1,0:T(8,128)}, f32[4,256,256]{2,1,0:T(8,128)}, u32[]{:S(2)}, u32[]{:S(2)}) %collective-permute-start.4) | collective-permute-done | bytes 1048608 | tf_op jit(solution)/shard_map/ppermute | solution.py:317
  98.7 2.1 %add_select_fusion.mine_ref = f32[4,256,256]{2,1,0:T(8,128)S(1)} fusion(f32[4,256,256]{2,1,0:T(8,128)} %get-tuple-element.44, f32[4,256,256]{2,1,0:T(8,128)S(1)} %collective-permute-done.6, f32[4,256,256]{2,1,0:T(8,128)} %collective-permute-done.4, f32[4,256,256]{2,1,0:T(8,128)} %collective-permute-done.5, pred[]{:T(512)S(6)} %lt.3), kind=kLoop, calls=%fused_computation | loop fusion | flops 786432 | bytes 5242881 | tf_op jit(solution)/shard_map/jit(_where)/select_n | solution.py:341
  100.8 1.5 %collective-permute-start.7 = (f32[4,256,256]{2,1,0:T(8,128)S(1)}, f32[4,256,256]{2,1,0:T(8,128)S(1)}, u32[]{:S(2)}, u32[]{:S(2)}) collective-permute-start(f32[4,256,256]{2,1,0:T(8,128)S(1)} %add_select_fusion.mine_ref), channel_id=1, source_target_pairs={{0,16},{16,0},{32,48},{48,32},{64,80},{80,64},{96,112},{112,96},{1... | collective-permute-start | bytes 3145736 | tf_op jit(solution)/shard_map/ppermute | solution.py:342
  102.3 0.1 pad_add_fusion.place
  102.4 2.2 %collective-permute-done.7.other_ref = f32[4,256,256]{2,1,0:T(8,128)S(1)} collective-permute-done((f32[4,256,256]{2,1,0:T(8,128)S(1)}, f32[4,256,256]{2,1,0:T(8,128)S(1)}, u32[]{:S(2)}, u32[]{:S(2)}) %collective-permute-start.7) | collective-permute-done | bytes 1048608 | tf_op jit(solution)/shard_map/ppermute | solution.py:342
  104.6 0.0 all-gather.3.cloned.1.call-done
  104.6 16.0 %shard_map.19 = f32[2048,8,128]{2,1,0:T(8,128)} custom-call(s32[2]{0:T(128)S(1)} %pad_add_fusion.place, f32[2048,8,128]{2,1,0:T(8,128)} %bitcast.14, f32[16,256,256]{2,1,0:T(8,128)} %bitcast.15, f32[256,256]{1,0:T(8,128)S(1)} %get-tuple-element.43.w0_ref, f32[256,256]{1,0:T(8,128)S(1)} %get-tuple-element.46.w1_ref, ...), custom_call_target="tpu_custom_call" | custom-call | tf_op jit(solution)/shard_map/pallas_call | solution.py:287
  (4 shorter events, 0.0 us)
Async XLA Ops:
  6.5 98.1 %all-gather.3.cloned.1.call-start = ((), (), s32[]{:S(2)}) async-start(), calls=%async_computation.3 | async-start | bytes 4456448 | tf_op jit(solution)/shard_map/all_gather | solution.py:331
  9.3 32.3 %collective-permute-start = (f32[256,256]{1,0:T(8,128)}, f32[256,256]{1,0:T(8,128)S(1)}, u32[]{:S(2)}, u32[]{:S(2)}) collective-permute-start(f32[256,256]{1,0:T(8,128)} %get-tuple-element.29), channel_id=1, source_target_pairs={{0,0},{1,17},{2,34},{3,51},{4,68},{5,85},{6,102},{7,119},{8,8},{9,... | collective-permute-start | bytes 786440 | tf_op jit(solution)/shard_map/ppermute | solution.py:326
  14.0 27.7 %collective-permute-start.1 = (f32[256,256]{1,0:T(8,128)}, f32[256,256]{1,0:T(8,128)S(1)}, u32[]{:S(2)}, u32[]{:S(2)}) collective-permute-start(f32[256,256]{1,0:T(8,128)} %get-tuple-element.30), channel_id=1, source_target_pairs={{0,2},{1,19},{2,32},{3,49},{4,70},{5,87},{6,100},{7,117},{8,10},{9... | collective-permute-start | bytes 786440 | tf_op jit(solution)/shard_map/ppermute | solution.py:326
  18.7 23.0 %collective-permute-start.2 = (f32[256,256]{1,0:T(8,128)}, f32[256,256]{1,0:T(8,128)S(1)}, u32[]{:S(2)}, u32[]{:S(2)}) collective-permute-start(f32[256,256]{1,0:T(8,128)} %get-tuple-element.31), channel_id=1, source_target_pairs={{0,4},{1,21},{2,38},{3,55},{4,72},{5,89},{6,106},{7,123},{8,12},{9... | collective-permute-start | bytes 786440 | tf_op jit(solution)/shard_map/ppermute | solution.py:326
  22.5 19.1 %collective-permute-start.3 = (f32[256,256]{1,0:T(8,128)}, f32[256,256]{1,0:T(8,128)S(1)}, u32[]{:S(2)}, u32[]{:S(2)}) collective-permute-start(f32[256,256]{1,0:T(8,128)} %get-tuple-element.32), channel_id=1, source_target_pairs={{0,6},{1,23},{2,36},{3,53},{4,74},{5,91},{6,104},{7,121},{8,14},{9... | collective-permute-start | bytes 786440 | tf_op jit(solution)/shard_map/ppermute | solution.py:326
  51.1 45.0 %collective-permute-start.6 = (f32[4,256,256]{2,1,0:T(8,128)}, f32[4,256,256]{2,1,0:T(8,128)S(1)}, u32[]{:S(2)}, u32[]{:S(2)}) collective-permute-start(f32[4,256,256]{2,1,0:T(8,128)} %get-tuple-element.44), channel_id=1, source_target_pairs={{0,64},{16,80},{1,65},{17,81},{2,66},{18,82},{3,67},{19,83},{4,68}... | collective-permute-start | bytes 3145736 | tf_op jit(solution)/shard_map/ppermute | solution.py:317
  53.9 42.2 %collective-permute-start.5 = (f32[4,256,256]{2,1,0:T(8,128)}, f32[4,256,256]{2,1,0:T(8,128)}, u32[]{:S(2)}, u32[]{:S(2)}) collective-permute-start(f32[4,256,256]{2,1,0:T(8,128)} %get-tuple-element.44), channel_id=1, source_target_pairs={{0,96},{16,112},{1,97},{17,113},{2,98},{18,114},{3,99},{19,115},{4... | collective-permute-start | bytes 3145736 | tf_op jit(solution)/shard_map/ppermute | solution.py:317
  56.2 42.5 %collective-permute-start.4 = (f32[4,256,256]{2,1,0:T(8,128)}, f32[4,256,256]{2,1,0:T(8,128)}, u32[]{:S(2)}, u32[]{:S(2)}) collective-permute-start(f32[4,256,256]{2,1,0:T(8,128)} %get-tuple-element.44), channel_id=1, source_target_pairs={{0,32},{16,48},{1,33},{17,49},{2,34},{18,50},{3,35},{19,51},{4,36}... | collective-permute-start | bytes 3145736 | tf_op jit(solution)/shard_map/ppermute | solution.py:317
  59.4 16.8 %all-to-all-start.2 = ((f32[16,3,16,256]{3,2,1,0:T(8,128)}), f32[16,3,16,256]{3,2,1,0:T(8,128)S(1)}, u32[]{:S(2)}, u32[]{:S(2)}) async-start(f32[16,3,16,256]{3,2,1,0:T(8,128)} %broadcast_in_dim.5), calls=%async_computation.2 | async-start | bytes 1572864 | tf_op jit(solution)/shard_map/all_to_all | solution.py:337
  100.8 3.8 %collective-permute-start.7 = (f32[4,256,256]{2,1,0:T(8,128)S(1)}, f32[4,256,256]{2,1,0:T(8,128)S(1)}, u32[]{:S(2)}, u32[]{:S(2)}) collective-permute-start(f32[4,256,256]{2,1,0:T(8,128)S(1)} %add_select_fusion.mine_ref), channel_id=1, source_target_pairs={{0,16},{16,0},{32,48},{48,32},{64,80},{80,64},{96,112},{112,96},{1... | collective-permute-start | bytes 3145736 | tf_op jit(solution)/shard_map/ppermute | solution.py:342
Sparse Core Ops, SparseCore 0:
  42.6 52.1 all-gather.2
